TPU v7x, 512 devices: a whole 4x8x8 slice. The times are simulated.
512 devices in a mesh: gx: 64 (over y, z), gy: 8 (over x, core).
Axes of the slice: x: 4, y: 8, z: 8, core: 2. Of those that a mesh axis runs over, the one named last changes fastest.
Arguments:
- right_border: float32 [5, 64, 128, 256], P(None, 'gx', 'gy'), may hold values from -8 to 8
- left_border: float32 [5, 64, 128, 256], P(None, 'gx', 'gy'), may hold values from -8 to 8
- velocity: float32 [3, 64, 128, 256], P(None, 'gx', 'gy'), may hold values from -5 to 5
- reaction: float32 [5, 64, 128, 256], P(None, 'gx', 'gy'), may hold values from 0.5 to 4
- diffusivity: float32 [5], replicated, may hold values from 0.5 to 2
- coupling: float32 [5, 5], replicated, may hold values from -3 to 3
Outputs:
- right_vector: float32 [5, 64, 128, 256], P(None, 'gx', 'gy')
- left_vector: float32 [5, 64, 128, 256], P(None, 'gx', 'gy')
All inputs are finite; a program needn't handle non-finite values.
Results may differ from a plain program's by a relative error of at most 0.0029.
Values sent between devices are 32-bit elements; how exact they have to be, the bound alone decides.
No kernel may reach another device: no remote copies, remote signals or barrier semaphores. Data moves between devices by JAX's collectives and lax.ppermute only.
A program may use at most 64 MiB of HBM per device.

v0:
```python
import jax
import jax.numpy as jnp
from jax import lax
from jax.sharding import PartitionSpec as P

ITERS = 2


CENTER = 8.0 / 3.0
EDGE = -1.0 / 6.0
CORNER = -1.0 / 12.0


def extended_2(block, sides, width):
    for axis, dim in sides:
        count = lax.axis_size(axis)
        forward = [(i, i + 1) for i in range(count - 1)]
        forward.append((count - 1, 0))
        backward = [(target, source) for source, target in forward]
        low = lax.ppermute(
            lax.slice_in_dim(block, block.shape[dim] - width, None, axis=dim), axis, forward
        )
        high = lax.ppermute(lax.slice_in_dim(block, 0, width, axis=dim), axis, backward)
        block = jnp.concatenate([low, block, high], axis=dim)
    return block


def add_depth(vec_field):
    return jnp.pad(vec_field, ((0, 0), (0, 0), (0, 0), (1, 1)))


def beside_all(extended, shift_x, shift_y, shift_z):
    return extended[
        :,
        1 + shift_x : extended.shape[1] - 1 + shift_x,
        1 + shift_y : extended.shape[2] - 1 + shift_y,
        1 + shift_z : extended.shape[3] - 1 + shift_z,
    ]


def laplace(extended):
    summed = CENTER * beside_all(extended, 0, 0, 0)
    for shift_x in (-1, 0, 1):
        for shift_y in (-1, 0, 1):
            for shift_z in (-1, 0, 1):
                offsets = abs(shift_x) + abs(shift_y) + abs(shift_z)
                if offsets == 2:
                    summed = summed + EDGE * beside_all(extended, shift_x, shift_y, shift_z)
                elif offsets == 3:
                    summed = summed + CORNER * beside_all(extended, shift_x, shift_y, shift_z)
    return summed


def forward_local(extended, velocity, reaction, diffusivity, coupling):
    center = beside_all(extended, 0, 0, 0)
    result = diffusivity[:, None, None, None] * laplace(extended)
    drift_sum = velocity[0:1] * (beside_all(extended, 1, 0, 0) - beside_all(extended, -1, 0, 0))
    drift_sum = drift_sum + velocity[1:2] * (
        beside_all(extended, 0, 1, 0) - beside_all(extended, 0, -1, 0)
    )
    drift_sum = drift_sum + velocity[2:3] * (
        beside_all(extended, 0, 0, 1) - beside_all(extended, 0, 0, -1)
    )
    mixing = jnp.einsum("cd,dxyz->cxyz", coupling, center, precision=lax.Precision.HIGHEST)
    return result + 0.5 * drift_sum + reaction * center + mixing


def adjoint_local(extended, flux_x, flux_y, flux_z, reaction, diffusivity, coupling):
    center = beside_all(extended, 0, 0, 0)
    result = diffusivity[:, None, None, None] * laplace(extended)
    drift_sum = beside_all(flux_x, 1, 0, 0) - beside_all(flux_x, -1, 0, 0)
    drift_sum = drift_sum + (beside_all(flux_y, 0, 1, 0) - beside_all(flux_y, 0, -1, 0))
    drift_sum = drift_sum + (flux_z[:, :, :, 2:] - flux_z[:, :, :, :-2])
    mixing = jnp.einsum("dc,dxyz->cxyz", coupling, center, precision=lax.Precision.HIGHEST)
    return result - 0.5 * drift_sum + reaction * center + mixing


def solve_small(start_len, columns):
    column_count = len(columns)
    hessenberg = jnp.zeros((column_count + 1, column_count), jnp.float32)
    for column, (coeffs, length) in enumerate(columns):
        hessenberg = hessenberg.at[: column + 1, column].set(coeffs)
        hessenberg = hessenberg.at[column + 1, column].set(length)
    normal = jnp.dot(hessenberg.T, hessenberg, precision=lax.Precision.HIGHEST)
    target = start_len * hessenberg[0]
    rows_list = [normal[row] for row in range(column_count)]
    rhs_list = [target[row] for row in range(column_count)]
    for pivot in range(column_count):
        for lower in range(pivot + 1, column_count):
            factor = rows_list[lower][pivot] / rows_list[pivot][pivot]
            rows_list[lower] = rows_list[lower] - factor * rows_list[pivot]
            rhs_list[lower] = rhs_list[lower] - factor * rhs_list[pivot]
    answer = [None] * column_count
    for pivot in range(column_count - 1, -1, -1):
        summed = rhs_list[pivot]
        for upper in range(pivot + 1, column_count):
            summed = summed - rows_list[pivot][upper] * answer[upper]
        answer[pivot] = summed / rows_list[pivot][pivot]
    return answer


def combine_basis(start_len, columns, krylov_basis):
    answer = solve_small(start_len, columns)
    result = answer[0] * krylov_basis[0]
    result = result + answer[1] * krylov_basis[1]
    return result


def local_terms(krylov_basis, mapped):
    dots = [jnp.sum(member * mapped) for member in krylov_basis]
    return jnp.stack(dots)


def project_out(mapped, coeffs, krylov_basis):
    for member_pos in range(len(krylov_basis)):
        mapped = mapped - coeffs[member_pos] * krylov_basis[member_pos]
    return mapped


def lengths_of(mapped_list):
    squares = jnp.stack([jnp.sum(member * member) for member in mapped_list])
    return jnp.sqrt(lax.psum(squares, ("gx", "gy")))


def krylov(first_vec, apply_fn):
    start_len = jnp.sqrt(lax.psum(jnp.sum(first_vec * first_vec), ("gx", "gy")))
    krylov_basis = [first_vec / start_len]
    columns = []
    for iteration in range(ITERS):
        mapped = apply_fn(krylov_basis[-1])
        totals = lax.psum(local_terms(krylov_basis, mapped), ("gx", "gy"))
        mapped = project_out(mapped, totals, krylov_basis)
        length = lengths_of([mapped])[0]
        columns.append((totals, length))
        krylov_basis.append(mapped / length)
    return combine_basis(start_len, columns, krylov_basis)


def per_device(right_border, left_border, velocity, reaction, diffusivity, coupling):
    comps = right_border.shape[0]

    def adjoint_from(adjoint_ext, flux_x, flux_y, vec_field):
        flux_z = add_depth(velocity[2:3] * vec_field)
        return adjoint_local(adjoint_ext, flux_x, flux_y, flux_z, reaction, diffusivity, coupling)

    def forward_apply(vec_field):
        extended = add_depth(extended_2(vec_field, (("gx", 1), ("gy", 2)), 1))
        return forward_local(extended, velocity, reaction, diffusivity, coupling)

    def adjoint_apply(vec_field):
        stacked = jnp.concatenate(
            [vec_field, velocity[0:1] * vec_field, velocity[1:2] * vec_field], 0
        )
        joined_ext = add_depth(extended_2(stacked, (("gx", 1), ("gy", 2)), 1))
        adjoint_ext = joined_ext[0:comps]
        flux_x = joined_ext[comps : 2 * comps]
        flux_y = joined_ext[2 * comps : 3 * comps]
        return adjoint_from(adjoint_ext, flux_x, flux_y, vec_field)

    right_vector = krylov(right_border, forward_apply)
    left_vector = krylov(left_border, adjoint_apply)
    return (right_vector, left_vector)


def solution(mesh):
    return jax.shard_map(
        per_device,
        mesh=mesh,
        in_specs=(
            P(None, "gx", "gy", None),
            P(None, "gx", "gy", None),
            P(None, "gx", "gy", None),
            P(None, "gx", "gy", None),
            P(),
            P(),
        ),
        out_specs=(P(None, "gx", "gy", None), P(None, "gx", "gy", None)),
        check_vma=False,
    )
```

profile of v0, /device:TPU:1, one launch (start us, length us, event | category | flops | bytes accessed | tf_op | source)
XLA Modules:
  0.0 601.4 jit_solution(2798396154743828533)
XLA Ops:
  0.6 1.6 multiply_reduce_fusion.10
  2.2 106.1 %all-reduce.12 = (f32[]{:T(128)}, f32[]{:T(128)}) all-reduce(f32[]{:T(128)} %get-tuple-element.156, f32[]{:T(128)} %get-tuple-element.155), channel_id=1, replica_groups=mesh['gx'=64,'gy'=8] {'gx','gy'}, use_global_device_ids=true, to_apply=%region_1.0 | all-reduce | flops 2 | bytes 16 | tf_op jit(solution)/shard_map/psum | solution.py:126
  109.0 0.9 copy_divide_fusion.1
  110.0 1.9 collective-permute-start
  111.9 6.7 %collective-permute-start.1 = (f32[5,1,16,256]{3,0,2,1:T(8,128)S(1)}, f32[5,1,16,256]{3,0,2,1:T(8,128)S(1)}, u32[]{:S(2)}, u32[]{:S(2)}) collective-permute-start(f32[5,1,16,256]{3,0,2,1:T(8,128)S(1)} %copy_divide_fusion.1), channel_id=1, source_target_pairs={{8,0},{16,8},{24,16},{32,24},{40,32},{48,40},{56,48},{64,56},{72,6... | collective-permute-start | bytes 245768 | tf_op jit(solution)/shard_map/ppermute | solution.py:23
  119.3 0.8 slice_bitcast_fusion.2
  120.0 1.0 broadcast_multiply_fusion.5
  121.1 2.1 collective-permute-start.8
  123.2 6.7 %collective-permute-start.9 = (f32[15,1,16,256]{3,0,2,1:T(8,128)S(1)}, f32[15,1,16,256]{3,0,2,1:T(8,128)S(1)}, u32[]{:S(2)}, u32[]{:S(2)}) collective-permute-start(f32[15,1,16,256]{3,0,2,1:T(8,128)S(1)} %pad_maximum_fusion), channel_id=1, source_target_pairs={{8,0},{16,8},{24,16},{32,24},{40,32},{48,40},{56,48},{64,56},{72,6... | collective-permute-start | bytes 737288 | tf_op jit(solution)/shard_map/ppermute | solution.py:23
  129.9 2.3 collective-permute-start.2
  132.2 0.7 fusion.134
  132.8 0.7 compare_reduce_fusion
  133.5 2.2 collective-permute-done.3
  136.0 0.8 collective-permute-start.10
  136.9 1.2 multiply_reduce_fusion.9
  138.1 2.6 collective-permute-done.11
  141.2 1.2 multiply_reduce_fusion.4
  142.5 99.8 %all-reduce.11 = (f32[1]{0:T(128)}, f32[1]{0:T(128)}) all-reduce(f32[1]{0:T(128)} %bitcast.7, f32[1]{0:T(128)} %bitcast.35), channel_id=1, replica_groups=mesh['gx'=64,'gy'=8] {'gx','gy'}, use_global_device_ids=true, to_apply=%region_3.4 | all-reduce | flops 2 | bytes 16 | tf_op jit(solution)/shard_map/psum | solution.py:131
  242.2 1.3 multiply_reduce_fusion.3
  243.5 1.3 multiply_reduce_fusion.8
  244.8 94.5 %all-reduce.10 = (f32[1]{0:T(128)}, f32[1]{0:T(128)}) all-reduce(f32[1]{0:T(128)} %bitcast.10, f32[1]{0:T(128)} %bitcast.38), channel_id=1, replica_groups=mesh['gx'=64,'gy'=8] {'gx','gy'}, use_global_device_ids=true, to_apply=%region_5.6 | all-reduce | flops 2 | bytes 16 | tf_op jit(solution)/shard_map/psum | solution.py:122
  340.0 0.7 broadcast_divide_fusion.1
  340.7 1.9 collective-permute-start.4
  342.6 6.7 %collective-permute-start.5 = (f32[5,1,16,256]{3,0,2,1:T(8,128)S(1)}, f32[5,1,16,256]{3,0,2,1:T(8,128)S(1)}, u32[]{:S(2)}, u32[]{:S(2)}) collective-permute-start(f32[5,1,16,256]{3,0,2,1:T(8,128)S(1)} %broadcast_divide_fusion.1), channel_id=1, source_target_pairs={{8,0},{16,8},{24,16},{32,24},{40,32},{48,40},{56,48},{64,56},{72,6... | collective-permute-start | bytes 245768 | tf_op jit(solution)/shard_map/ppermute | solution.py:23
  350.0 0.7 broadcast_multiply_fusion.4
  351.3 3.5 collective-permute-start.6
  354.8 1.9 collective-permute-start.12
  356.7 7.4 %collective-permute-start.13 = (f32[15,1,16,256]{3,0,2,1:T(8,128)S(1)}, f32[15,1,16,256]{3,0,2,1:T(8,128)S(1)}, u32[]{:S(2)}, u32[]{:S(2)}) collective-permute-start(f32[15,1,16,256]{3,0,2,1:T(8,128)S(1)} %pad_maximum_fusion.1), channel_id=1, source_target_pairs={{8,0},{16,8},{24,16},{32,24},{40,32},{48,40},{56,48},{64,56},{72,6... | collective-permute-start | bytes 737288 | tf_op jit(solution)/shard_map/ppermute | solution.py:23
  364.1 0.7 scatter.34
  365.8 1.2 multiply_reduce_fusion.7
  367.5 0.9 collective-permute-done.13
  368.4 2.2 collective-permute-start.14
  370.7 1.4 pad_maximum_fusion.50
  372.0 2.4 collective-permute-done.15
  375.0 1.3 multiply_reduce_fusion.2
  376.3 1.4 pad_maximum_fusion.51
  377.8 100.2 %all-reduce.9 = (f32[2]{0:T(128)S(1)}, f32[2]{0:T(128)S(1)}) all-reduce(f32[2]{0:T(128)S(1)} %pad_maximum_fusion.50, f32[2]{0:T(128)S(1)} %pad_maximum_fusion.51), channel_id=1, replica_groups=mesh['gx'=64,'gy'=8] {'gx','gy'}, use_global_device_ids=true, to_apply=%region_9.10 | all-reduce | flops 4 | bytes 32 | tf_op jit(solution)/shard_map/psum | solution.py:131
  478.6 2.0 broadcast_select_fusion
  480.5 1.4 scatter.36
  482.5 2.0 multiply_reduce_fusion
  484.5 2.0 multiply_reduce_fusion.5
  486.5 94.3 %all-reduce.8 = (f32[1]{0:T(128)}, f32[1]{0:T(128)}) all-reduce(f32[1]{0:T(128)} %bitcast.23, f32[1]{0:T(128)} %bitcast.50), channel_id=1, replica_groups=mesh['gx'=64,'gy'=8] {'gx','gy'}, use_global_device_ids=true, to_apply=%region_11.12 | all-reduce | flops 2 | bytes 16 | tf_op jit(solution)/shard_map/psum | solution.py:122
  582.4 2.0 broadcast_select_fusion.1
  584.3 1.4 scatter.30
  586.0 0.7 fusion.128
  593.0 0.7 copy.17
  593.7 0.7 fusion.130
  600.8 0.7 copy.16
  (57 shorter events, 7.8 us)
Async XLA Ops:
  0.6 136.2 %copy-start = (f32[5,5]{1,0:T(8,128)S(1)}, f32[5,5]{1,0:T(8,128)}, u32[]{:S(2)}) copy-start(f32[5,5]{1,0:T(8,128)} %param.27) | copy-start | bytes 304
  110.0 19.9 %collective-permute-start = (f32[5,1,16,256]{3,0,2,1:T(8,128)S(1)}, f32[5,1,16,256]{3,0,2,1:T(8,128)S(1)}, u32[]{:S(2)}, u32[]{:S(2)}) collective-permute-start(f32[5,1,16,256]{3,0,2,1:T(8,128)S(1)} %copy_divide_fusion.1), channel_id=1, source_target_pairs={{0,8},{8,16},{16,24},{24,32},{32,40},{40,48},{48,56},{56,64},{64,7... | collective-permute-start | bytes 245768 | tf_op jit(solution)/shard_map/ppermute | solution.py:20
  111.9 18.0 %collective-permute-start.1 = (f32[5,1,16,256]{3,0,2,1:T(8,128)S(1)}, f32[5,1,16,256]{3,0,2,1:T(8,128)S(1)}, u32[]{:S(2)}, u32[]{:S(2)}) collective-permute-start(f32[5,1,16,256]{3,0,2,1:T(8,128)S(1)} %copy_divide_fusion.1), channel_id=1, source_target_pairs={{8,0},{16,8},{24,16},{32,24},{40,32},{48,40},{56,48},{64,56},{72,6... | collective-permute-start | bytes 245768 | tf_op jit(solution)/shard_map/ppermute | solution.py:23
  121.1 15.8 %copy-start.2 = (f32[5,1,16,256]{3,2,1,0:T(8,128)S(1)}, f32[5,1,16,256]{3,2,1,0:T(8,128)}, u32[]{:S(2)}) copy-start(f32[5,1,16,256]{3,2,1,0:T(8,128)} %param.22) | copy-start | bytes 245764
  121.1 15.8 %copy-start.3 = (f32[5,1,16,256]{3,2,1,0:T(8,128)S(1)}, f32[5,1,16,256]{3,2,1,0:T(8,128)}, u32[]{:S(2)}) copy-start(f32[5,1,16,256]{3,2,1,0:T(8,128)} %param.25) | copy-start | bytes 245764
  121.1 15.8 %copy-start.4 = (f32[5]{0:T(128)S(1)}, f32[5]{0:T(128)}, u32[]{:S(2)}) copy-start(f32[5]{0:T(128)} %param.26) | copy-start | bytes 64
  121.1 14.9 %collective-permute-start.8 = (f32[15,1,16,256]{3,0,2,1:T(8,128)S(1)}, f32[15,1,16,256]{3,0,2,1:T(8,128)S(1)}, u32[]{:S(2)}, u32[]{:S(2)}) collective-permute-start(f32[15,1,16,256]{3,0,2,1:T(8,128)S(1)} %pad_maximum_fusion), channel_id=1, source_target_pairs={{0,8},{8,16},{16,24},{24,32},{32,40},{40,48},{48,56},{56,64},{64,7... | collective-permute-start | bytes 737288 | tf_op jit(solution)/shard_map/ppermute | solution.py:20
  123.2 12.8 %collective-permute-start.9 = (f32[15,1,16,256]{3,0,2,1:T(8,128)S(1)}, f32[15,1,16,256]{3,0,2,1:T(8,128)S(1)}, u32[]{:S(2)}, u32[]{:S(2)}) collective-permute-start(f32[15,1,16,256]{3,0,2,1:T(8,128)S(1)} %pad_maximum_fusion), channel_id=1, source_target_pairs={{8,0},{16,8},{24,16},{32,24},{40,32},{48,40},{56,48},{64,56},{72,6... | collective-permute-start | bytes 737288 | tf_op jit(solution)/shard_map/ppermute | solution.py:23
  129.9 3.6 collective-permute-start.2
  132.2 3.5 collective-permute-start.3
  136.0 2.1 collective-permute-start.10
  136.9 3.8 collective-permute-start.11
  138.1 3.2 copy-start.1
  340.7 10.1 %collective-permute-start.4 = (f32[5,1,16,256]{3,0,2,1:T(8,128)S(1)}, f32[5,1,16,256]{3,0,2,1:T(8,128)S(1)}, u32[]{:S(2)}, u32[]{:S(2)}) collective-permute-start(f32[5,1,16,256]{3,0,2,1:T(8,128)S(1)} %broadcast_divide_fusion.1), channel_id=1, source_target_pairs={{0,8},{8,16},{16,24},{24,32},{32,40},{40,48},{48,56},{56,64},{64,7... | collective-permute-start | bytes 245768 | tf_op jit(solution)/shard_map/ppermute | solution.py:20
  342.6 8.6 %collective-permute-start.5 = (f32[5,1,16,256]{3,0,2,1:T(8,128)S(1)}, f32[5,1,16,256]{3,0,2,1:T(8,128)S(1)}, u32[]{:S(2)}, u32[]{:S(2)}) collective-permute-start(f32[5,1,16,256]{3,0,2,1:T(8,128)S(1)} %broadcast_divide_fusion.1), channel_id=1, source_target_pairs={{8,0},{16,8},{24,16},{32,24},{40,32},{48,40},{56,48},{64,56},{72,6... | collective-permute-start | bytes 245768 | tf_op jit(solution)/shard_map/ppermute | solution.py:23
  351.3 14.3 %collective-permute-start.6 = (f32[5,3,1,256]{3,0,2,1:T(8,128)S(1)}, f32[5,3,1,256]{3,0,2,1:T(8,128)S(1)}, u32[]{:S(2)}, u32[]{:S(2)}) collective-permute-start(f32[5,3,1,256]{3,0,2,1:T(8,128)S(1)} %get-tuple-element.120), channel_id=1, source_target_pairs={{0,1},{1,2},{2,3},{3,4},{4,5},{5,6},{6,7},{7,0},{8,9},{9,10},{10,1... | collective-permute-start | bytes 46088 | tf_op jit(solution)/shard_map/ppermute | solution.py:20
  354.7 10.9 %collective-permute-start.7 = (f32[5,3,1,256]{3,0,2,1:T(8,128)S(1)}, f32[5,3,1,256]{3,0,2,1:T(8,128)S(1)}, u32[]{:S(2)}, u32[]{:S(2)}) collective-permute-start(f32[5,3,1,256]{3,0,2,1:T(8,128)S(1)} %get-tuple-element.121), channel_id=1, source_target_pairs={{1,0},{2,1},{3,2},{4,3},{5,4},{6,5},{7,6},{0,7},{9,8},{10,9},{11,1... | collective-permute-start | bytes 46088 | tf_op jit(solution)/shard_map/ppermute | solution.py:23
  354.8 12.7 %collective-permute-start.12 = (f32[15,1,16,256]{3,0,2,1:T(8,128)S(1)}, f32[15,1,16,256]{3,0,2,1:T(8,128)S(1)}, u32[]{:S(2)}, u32[]{:S(2)}) collective-permute-start(f32[15,1,16,256]{3,0,2,1:T(8,128)S(1)} %pad_maximum_fusion.1), channel_id=1, source_target_pairs={{0,8},{8,16},{16,24},{24,32},{32,40},{40,48},{48,56},{56,64},{64,7... | collective-permute-start | bytes 737288 | tf_op jit(solution)/shard_map/ppermute | solution.py:20
  356.7 11.7 %collective-permute-start.13 = (f32[15,1,16,256]{3,0,2,1:T(8,128)S(1)}, f32[15,1,16,256]{3,0,2,1:T(8,128)S(1)}, u32[]{:S(2)}, u32[]{:S(2)}) collective-permute-start(f32[15,1,16,256]{3,0,2,1:T(8,128)S(1)} %pad_maximum_fusion.1), channel_id=1, source_target_pairs={{8,0},{16,8},{24,16},{32,24},{40,32},{48,40},{56,48},{64,56},{72,6... | collective-permute-start | bytes 737288 | tf_op jit(solution)/shard_map/ppermute | solution.py:23
  368.4 3.6 collective-permute-start.14
  370.7 3.8 collective-permute-start.15
where the time goes:
time: 603 us; the launch traced here: 601 us
  blocking collectives  495 us (82%)
  starting transfers between devices  44.1 us (7%)
  other arithmetic  20.6 us (3%)
  between operations  15.4 us (3%)
  local copies, waits for them, and re-layouts  12.2 us (2%)
  waiting for transfers between devices  9.15 us (2%)
    psum x2, blocking collectives, krylov(): totals = lax.psum(local_terms(krylov_basis, mapped), ('gx', 'gy'))  200 us
    psum x2, blocking collectives, lengths_of(): return jnp.sqrt(lax.psum(squares, ('gx', 'gy')))  189 us
    psum x1, blocking collectives, krylov(): start_len = jnp.sqrt(lax.psum(jnp.sum(first_vec * first_vec), ('gx', 'gy')))  106 us
    ppermute x8, starting transfers between devices, extended_2(): lax.ppermute(lax.slice_in_dim(block, 0, width, axis=dim), axis, backward)  27.5 us
    ppermute x8, starting transfers between devices, extended_2(): lax.ppermute(lax.slice_in_dim(block, block.shape[dim] - width, None, axis...  16.6 us
  transfers between devices with their start and end apart: 16, of which 6 were waited for; matrix products, arithmetic and copies ran while one was open for 2% of the time, Pallas kernels for 0%

commit v1 on v0

v1 whole, which is shorter than its diff:
```python
import functools

import jax
import jax.numpy as jnp
from jax import lax
from jax.experimental import pallas as pl
from jax.experimental.pallas import tpu as pltpu
from jax.sharding import PartitionSpec as P

CENTER = 8.0 / 3.0
EDGE = -1.0 / 6.0

COMPS = 5
FIELDS = 2 * COMPS
SUMS = 5


def up(v):
    size = v.shape[-1]
    lane = lax.broadcasted_iota(jnp.int32, v.shape, v.ndim - 1)
    return jnp.where(lane == size - 1, 0.0, pltpu.roll(v, size - 1, v.ndim - 1))


def down(v):
    lane = lax.broadcasted_iota(jnp.int32, v.shape, v.ndim - 1)
    return jnp.where(lane == 0, 0.0, pltpu.roll(v, 1, v.ndim - 1))


def apply_both(rows, mid, even, odd, sign, vx, vy3, vz, vx_even, vx_odd, react, diff_ref, coup_ref):
    outs = []
    centers = [mid(f, 0) for f in range(FIELDS)]
    for f in range(FIELDS):
        c = f % COMPS
        right = f < COMPS
        b1, b0, b2 = centers[f], mid(f, -1), mid(f, 1)
        e1, o1 = even(f, 0), odd(f, 0)
        ya = (even(f, -1) + odd(f, -1)) + (even(f, 1) + odd(f, 1))
        t = (e1 + o1) + (b0 + b2) + 0.5 * ya
        d = diff_ref[c]
        base = (CENTER * d + react(c)) * b1
        if right:
            drift = (sign * vx) * (e1 - o1) + vy3[1] * (b2 - b0) + vz * (up(b1) - down(b1))
            out = base + (EDGE * d) * (ya + up(t) + down(t)) + 0.5 * drift
            for k in range(COMPS):
                out = out + coup_ref[c, k] * centers[k]
        else:
            fz = 0.5 * (vz * b1)
            g = (EDGE * d) * t
            drift = sign * (vx_even * e1 - vx_odd * o1) + (vy3[2] * b2 - vy3[0] * b0)
            out = base + (EDGE * d) * ya - 0.5 * drift + up(g - fz) + down(g + fz)
            for k in range(COMPS):
                out = out + coup_ref[k, c] * centers[COMPS + k]
        outs.append(out)
    return outs


def sign_here():
    return jnp.where(lax.rem(lax.axis_index("gx"), 2) == 0, 1.0, -1.0).astype(jnp.float32)


def first_kernel(ny, coup_ref, diff_ref, sr, sl, vel, rea, lo, hi, even, odd, out, field, coef):
    rows = ny + 8
    for f in range(FIELDS):
        src = sr if f < COMPS else sl
        field[0, f, 2 : ny + 2] = src[f % COMPS]
        field[0, f, 0:2] = lo[2 * f : 2 * f + 2]
        field[0, f, ny + 2 : ny + 4] = hi[2 * f : 2 * f + 2]
        for side, ref in ((1, even), (2, odd)):
            field[side, f, 2 : ny + 2] = ref[f * ny : (f + 1) * ny]
            at = FIELDS * ny + ny + 2 * f
            field[side, f, 0:2] = ref[at : at + 2]
            at = at + 2 * FIELDS
            field[side, f, ny + 2 : ny + 4] = ref[at : at + 2]
    halo = 2 * FIELDS
    for c in range(COMPS):
        coef[c, 1 : ny + 1] = rea[c]
        coef[c, 0:1] = lo[halo + c : halo + c + 1]
        coef[c, ny + 1 : ny + 2] = hi[halo + c : halo + c + 1]
    halo += COMPS
    for at, k, row in ((5, 0, halo), (6, 2, halo + 1)):
        coef[at, 1 : ny + 1] = vel[k]
        coef[at, 0:1] = lo[row : row + 1]
        coef[at, ny + 1 : ny + 2] = hi[row : row + 1]
    for at, ref in ((7, even), (8, odd)):
        coef[at, 1 : ny + 1] = ref[FIELDS * ny : FIELDS * ny + ny]
        last = FIELDS * ny + ny + 4 * FIELDS
        coef[at, 0:1] = ref[last : last + 1]
        coef[at, ny + 1 : ny + 2] = ref[last + 1 : last + 2]
    coef[9, 2 : ny + 2] = vel[1]
    coef[9, 0:2] = lo[halo + 2 : halo + 4]
    coef[9, ny + 2 : ny + 4] = hi[halo + 2 : halo + 4]

    def plane(side):
        return lambda f, shift: field[side, f, 1 + shift : 1 + shift + rows]

    outs = apply_both(
        rows, plane(0), plane(1), plane(2), sign_here(),
        coef[5, 0:rows], [coef[9, k : k + rows] for k in range(3)], coef[6, 0:rows],
        coef[7, 0:rows], coef[8, 0:rows], lambda c: coef[c, 0:rows], diff_ref, coup_ref,
    )
    for f in range(FIELDS):
        field[0, f, 0:rows] = outs[f]
        out[f * ny : (f + 1) * ny] = field[0, f, 1 : ny + 1]
        at = FIELDS * ny + 2 * f
        out[at : at + 1] = field[0, f, 0:1]
        out[at + 1 : at + 2] = field[0, f, ny + 1 : ny + 2]


def second_kernel(ny, copies, coup_ref, diff_ref, sr, sl, vel, rea, lo, hi, even1, odd1, own, even, odd, out, field, vys):
    for f in range(FIELDS):
        for side, ref in ((0, own), (1, even), (2, odd)):
            field[side, f, 1 : ny + 1] = ref[f * ny : (f + 1) * ny]
            at = FIELDS * ny + 2 * f
            field[side, f, 0:1] = ref[at : at + 1]
            field[side, f, ny + 1 : ny + 2] = ref[at + 1 : at + 2]
    row = 2 * FIELDS + COMPS + 2
    vys[1 : ny + 1] = vel[1]
    vys[0:1] = lo[row + 1 : row + 2]
    vys[ny + 1 : ny + 2] = hi[row : row + 1]

    def plane(side):
        return lambda f, shift: field[side, f, 1 + shift : 1 + shift + ny]

    at = FIELDS * ny
    outs = apply_both(
        ny, plane(0), plane(1), plane(2), sign_here(),
        vel[0], [vys[k : k + ny] for k in range(3)], vel[2],
        even1[at : at + ny], odd1[at : at + ny], lambda c: rea[c], diff_ref, coup_ref,
    )
    lane = lax.broadcasted_iota(jnp.int32, (1, 128), 1)
    total = jnp.zeros((1, 128), jnp.float32)
    for system, start in ((0, sr), (1, sl)):
        sums = [0.0] * SUMS
        for c in range(COMPS):
            f = system * COMPS + c
            s, w1, w2 = start[c], field[0, f, 1 : ny + 1], outs[f]
            for k, term in enumerate((w1 * w1, w1 * w2, w2 * w2, w1 * s, w2 * s)):
                sums[k] = sums[k] + term
        for k in range(SUMS):
            value = jnp.sum(jnp.sum(sums[k], axis=0, keepdims=True), axis=1, keepdims=True)
            total = total + jnp.where(lane == system * SUMS + k, value, 0.0)
    out[...] = jnp.broadcast_to(total, (copies, 128))


def last_kernel(ny, parts, sr, sl, own, out_r, out_l):
    total = jnp.sum(parts[...], axis=0, keepdims=True)
    lane = lax.broadcasted_iota(jnp.int32, (1, 128), 1)
    for system, start, out in ((0, sr, out_r), (1, sl, out_l)):
        g11, g12, g22, r1, r2 = [
            jnp.sum(jnp.where(lane == system * SUMS + k, total, 0.0), axis=1, keepdims=True)
            for k in range(SUMS)
        ]
        factor = g12 / g11
        b = (r2 - factor * r1) / (g22 - factor * g12)
        a = (r1 - g12 * b) / g11
        for c in range(COMPS):
            f = system * COMPS + c
            out[c] = a * start[c] + b * own[f * ny : (f + 1) * ny]


def per_device(right_border, left_border, velocity, reaction, diffusivity, coupling):
    comps, _, ny, nz = right_border.shape
    nx_count, ny_count = lax.axis_size("gx"), lax.axis_size("gy")
    f32 = jnp.float32
    sr, sl, vel, rea = (v.reshape(v.shape[0], ny, nz) for v in (right_border, left_border, velocity, reaction))

    def edge(two, one):
        pick = lambda v, where: v[..., where, :].reshape(-1, nz)
        return jnp.concatenate(
            [pick(sr, two), pick(sl, two), pick(rea, one), pick(vel[0:1], one), pick(vel[2:3], one), pick(vel[1:2], two)]
        )

    ahead = [(i, (i + 1) % ny_count) for i in range(ny_count)]
    back = [(j, i) for i, j in ahead]
    lo = lax.ppermute(edge(slice(ny - 2, ny), slice(ny - 1, ny)), "gy", ahead)
    hi = lax.ppermute(edge(slice(0, 2), slice(0, 1)), "gy", back)

    even_pairs = [(i, i ^ 1) for i in range(nx_count)]
    odd_pairs = [(i, (i - 1 if i % 2 == 0 else i + 1) % nx_count) for i in range(nx_count)]

    def swap(v):
        return lax.ppermute(v, "gx", even_pairs), lax.ppermute(v, "gx", odd_pairs)

    halo, vx_row = 2 * FIELDS, 2 * FIELDS + COMPS
    payload = jnp.concatenate(
        [
            sr.reshape(-1, nz), sl.reshape(-1, nz), vel[0], lo[:halo], hi[:halo],
            lo[vx_row : vx_row + 1], hi[vx_row : vx_row + 1],
        ]
    )
    even1, odd1 = swap(payload)

    smem, vmem = pl.BlockSpec(memory_space=pltpu.SMEM), pl.BlockSpec(memory_space=pltpu.VMEM)
    own = pl.pallas_call(
        functools.partial(first_kernel, ny),
        out_shape=jax.ShapeDtypeStruct((FIELDS * (ny + 2), nz), f32),
        in_specs=[smem] * 2 + [vmem] * 8,
        out_specs=vmem,
        scratch_shapes=[pltpu.VMEM((3, FIELDS, ny + 16, nz), f32), pltpu.VMEM((10, ny + 16, nz), f32)],
        name="first_product",
    )(coupling, diffusivity, sr, sl, vel, rea, lo, hi, even1, odd1)
    even2, odd2 = swap(own)
    shares = pl.pallas_call(
        functools.partial(second_kernel, ny, ny_count),
        out_shape=jax.ShapeDtypeStruct((ny_count, 128), f32),
        in_specs=[smem] * 2 + [vmem] * 11,
        out_specs=vmem,
        scratch_shapes=[pltpu.VMEM((3, FIELDS, ny + 8, nz), f32), pltpu.VMEM((ny + 8, nz), f32)],
        name="second_product",
    )(coupling, diffusivity, sr, sl, vel, rea, lo, hi, even1, odd1, own, even2, odd2)
    shares = lax.all_to_all(shares, "gy", 0, 0, tiled=True)
    shares = jnp.broadcast_to(jnp.sum(shares, axis=0, keepdims=True), (nx_count, 128))
    shares = lax.all_to_all(shares, "gx", 0, 0, tiled=True)
    right, left = pl.pallas_call(
        functools.partial(last_kernel, ny),
        out_shape=[jax.ShapeDtypeStruct((comps, ny, nz), f32)] * 2,
        in_specs=[vmem] * 4,
        out_specs=[vmem] * 2,
        name="combine",
    )(shares, sr, sl, own)
    return right.reshape(right_border.shape), left.reshape(left_border.shape)


def solution(mesh):
    block = P(None, "gx", "gy", None)
    return jax.shard_map(
        per_device,
        mesh=mesh,
        in_specs=(block, block, block, block, P(), P()),
        out_specs=(block, block),
        check_vma=False,
    )
```

time: 603 us -> 80.4 us (0.13)
  blocking collectives: 495 us -> 31.2 us
  other arithmetic: 20.6 us -> 0.03 us
  starting transfers between devices: 44.1 us -> 23.7 us
  between operations: 15.4 us -> 0.81 us
  Pallas kernels: 0 us -> 7.35 us
  local copies, waits for them, and re-layouts: 12.2 us -> 5.72 us
    psum x5 -> x0, blocking collectives: 495 us -> none  [the longest x2 200 us: krylov(): totals = lax.psum(local_terms(krylov_basis, mapped), ('gx', 'gy'))]
    all_to_all x0 -> x2, blocking collectives: none -> 31.2 us  [the longest x1 17.1 us: per_device(): shares = lax.all_to_all(shares, 'gx', 0, 0, tiled=True)]
    ppermute x16 -> x6, starting transfers between devices: 44.1 us -> 23.7 us  [the longest x4 16.8 us: swap(): return (lax.ppermute(v, 'gx', even_pairs), lax.ppermute(v, 'gx', odd_pairs))]
    reduce_sum x5 -> x1, other arithmetic: 8.11 us -> 0.03 us  [per_device(): jnp.sum(shares, axis=0, keepdims=True)]
    pallas_call x0 -> x3, Pallas kernels: none -> 7.35 us  [the longest x1 2.78 us: per_device(): pl.pallas_call(functools.partial(first_kernel, ny), out_shape=jax.ShapeDt...]
    another operation x5 -> x0, other arithmetic: 7.3 us -> none
  transfers between devices with their start and end apart: 16 -> 6, of which waited for: 6 -> 5; matrix products, arithmetic and copies ran while one was open for 2% -> 0% of each run, Pallas kernels for 0% -> 0%
where the time goes in v1:
time: 80.4 us; the launch traced here: 79.9 us
  blocking collectives  31.2 us (39%)
  starting transfers between devices  23.7 us (29%)
  waiting for transfers between devices  11.1 us (14%)
  Pallas kernels  7.35 us (9%)
  local copies, waits for them, and re-layouts  5.72 us (7%)
  between operations  0.81 us (1%)
    all_to_all x1, blocking collectives, per_device(): shares = lax.all_to_all(shares, 'gx', 0, 0, tiled=True)  17.1 us
    ppermute x4, starting transfers between devices, swap(): return (lax.ppermute(v, 'gx', even_pairs), lax.ppermute(v, 'gx', odd_pairs))  16.8 us
    all_to_all x1, blocking collectives, per_device(): shares = lax.all_to_all(shares, 'gy', 0, 0, tiled=True)  14.1 us
    ppermute x4, waiting for transfers between devices, swap(): return (lax.ppermute(v, 'gx', even_pairs), lax.ppermute(v, 'gx', odd_pairs))  9.95 us
    ppermute x1, starting transfers between devices, per_device(): hi = lax.ppermute(edge(slice(0, 2), slice(0, 1)), 'gy', back)  6.88 us
    unnamed x21, local copies, waits for them, and re-layouts  3.32 us
    pallas_call x1, Pallas kernels, per_device(): pl.pallas_call(functools.partial(first_kernel, ny), out_shape=jax.ShapeDt...  2.78 us
    pallas_call x1, Pallas kernels, per_device(): pl.pallas_call(functools.partial(second_kernel, ny, ny_count), out_shape=...  2.77 us
  transfers between devices with their start and end apart: 6, of which 5 were waited for; matrix products, arithmetic and copies ran while one was open for 0% of the time, Pallas kernels for 0%

profile of v1, /device:TPU:1, one launch (start us, length us, event | category | flops | bytes accessed | tf_op | source)
XLA Modules:
  0.0 79.9 jit_solution(16693402891503644855)
XLA Ops:
  0.6 0.8 %fusion.1 = (f32[5,2,256]{2,1,0:T(2,128)S(1)}, f32[5,2,256]{2,1,0:T(2,128)S(1)}) fusion(f32[5,16,256]{2,1,0:T(8,128)} %bitcast.43), kind=kLoop, calls=%fused_computation.14 | loop fusion | bytes 40960 | tf_op jit(solution)/shard_map/slice | solution.py:168
  1.4 0.0 copy-start.5
  1.5 0.8 %fusion = (f32[5,2,256]{2,1,0:T(2,128)S(1)}, f32[5,2,256]{2,1,0:T(2,128)S(1)}) fusion(f32[5,16,256]{2,1,0:T(8,128)} %bitcast.48), kind=kLoop, calls=%fused_computation.13 | loop fusion | bytes 40960 | tf_op jit(solution)/shard_map/slice | solution.py:168
  2.3 0.0 copy-start.4
  2.3 0.0 copy-done.5
  2.3 0.8 %copy-done.4 = f32[5,1,16,256]{3,2,1,0:T(8,128)S(1)} copy-done((f32[5,1,16,256]{3,2,1,0:T(8,128)S(1)}, f32[5,1,16,256]{3,2,1,0:T(8,128)}, u32[]{:S(2)}) %copy-start.4) | copy-done | bytes 81944
  3.2 0.1 copy.21
  3.2 0.3 concatenate.10
  3.5 6.9 %collective-permute-start.1 = (f32[29,256]{1,0:T(8,128)S(1)}, f32[29,256]{1,0:T(8,128)S(1)}, u32[]{:S(2)}, u32[]{:S(2)}) collective-permute-start(f32[29,256]{1,0:T(8,128)S(1)} %concatenate.10), channel_id=1, source_target_pairs={{1,0},{2,1},{3,2},{4,3},{5,4},{6,5},{7,6},{0,7},{9,8},{10,9},{11,1... | collective-permute-start | bytes 89096 | tf_op jit(solution)/shard_map/ppermute | solution.py:176
  10.4 0.0 copy-start
  10.4 0.0 copy-start.1
  10.4 0.3 concatenate.9
  10.7 0.0 collective-permute-start
  10.7 0.5 collective-permute-done.1.hi
  11.2 0.0 copy-start.6
  11.3 0.6 collective-permute-done.lo
  11.9 0.0 copy-start.7
  11.9 0.0 copy-done.6
  11.9 0.0 copy-done
  11.9 0.0 copy-done.1
  11.9 0.2 concatenate.11
  12.1 0.4 copy-done.7
  12.5 9.9 %collective-permute-start.3 = (f32[218,256]{1,0:T(8,128)S(1)}, f32[218,256]{1,0:T(8,128)S(1)}, u32[]{:S(2)}, u32[]{:S(2)}) collective-permute-start(f32[218,256]{1,0:T(8,128)S(1)} %concatenate.11), channel_id=1, source_target_pairs={{0,504},{8,16},{16,8},{24,32},{32,24},{40,48},{48,40},{56,64},{64,... | collective-permute-start | bytes 669704 | tf_op jit(solution)/shard_map/ppermute | solution.py:182
  22.4 1.9 %collective-permute-start.2 = (f32[218,256]{1,0:T(8,128)S(1)}, f32[218,256]{1,0:T(8,128)S(1)}, u32[]{:S(2)}, u32[]{:S(2)}) collective-permute-start(f32[218,256]{1,0:T(8,128)S(1)} %concatenate.11), channel_id=1, source_target_pairs={{0,8},{8,0},{16,24},{24,16},{32,40},{40,32},{48,56},{56,48},{64,72... | collective-permute-start | bytes 669704 | tf_op jit(solution)/shard_map/ppermute | solution.py:182
  24.3 1.5 %collective-permute-done.3.odd.odd1 = f32[218,256]{1,0:T(8,128)S(1)} collective-permute-done((f32[218,256]{1,0:T(8,128)S(1)}, f32[218,256]{1,0:T(8,128)S(1)}, u32[]{:S(2)}, u32[]{:S(2)}) %collective-permute-start.3) | collective-permute-done | bytes 223264 | tf_op jit(solution)/shard_map/ppermute | solution.py:182
  25.8 0.0 copy-start.2
  25.8 3.7 %collective-permute-done.2.even.even1 = f32[218,256]{1,0:T(8,128)S(1)} collective-permute-done((f32[218,256]{1,0:T(8,128)S(1)}, f32[218,256]{1,0:T(8,128)S(1)}, u32[]{:S(2)}, u32[]{:S(2)}) %collective-permute-start.2) | collective-permute-done | bytes 223264 | tf_op jit(solution)/shard_map/ppermute | solution.py:182
  29.5 0.0 copy-start.3
  29.5 0.0 copy-done.2
  29.5 0.7 copy-done.3
  30.1 2.8 %first_product.1.own = f32[180,256]{1,0:T(8,128)} custom-call(f32[5,5]{1,0:T(8,128)} %coup_ref.3, f32[5]{0:T(128)} %diff_ref.3, f32[5,16,256]{2,1,0:T(8,128)} %bitcast.44, f32[5,16,256]{2,1,0:T(8,128)} %bitcast.49, f32[3,16,256]{2,1,0:T(8,128)} %bitcast.55, f32[5,16,256]{2,1,0:T(8,128)} %bitcast.53, f32[29,256]{1,0:T(8,128)} %copy-done.7, ...), custom_call_target="tpu_custom_call" | custom-call | tf_op jit(solution)/shard_map/first_product/pallas_call | solution.py:194
  32.9 3.1 %collective-permute-start.5 = (f32[180,256]{1,0:T(8,128)}, f32[180,256]{1,0:T(8,128)S(1)}, u32[]{:S(2)}, u32[]{:S(2)}) collective-permute-start(f32[180,256]{1,0:T(8,128)} %first_product.1.own), channel_id=1, source_target_pairs={{0,504},{8,16},{16,8},{24,32},{32,24},{40,48},{48,40},{56,64},{64,... | collective-permute-start | bytes 552968 | tf_op jit(solution)/shard_map/ppermute | solution.py:182
  36.0 1.9 %collective-permute-start.4 = (f32[180,256]{1,0:T(8,128)}, f32[180,256]{1,0:T(8,128)S(1)}, u32[]{:S(2)}, u32[]{:S(2)}) collective-permute-start(f32[180,256]{1,0:T(8,128)} %first_product.1.own), channel_id=1, source_target_pairs={{0,8},{8,0},{16,24},{24,16},{32,40},{40,32},{48,56},{56,48},{64,72... | collective-permute-start | bytes 552968 | tf_op jit(solution)/shard_map/ppermute | solution.py:182
  37.9 4.8 %collective-permute-done.5.odd = f32[180,256]{1,0:T(8,128)S(1)} collective-permute-done((f32[180,256]{1,0:T(8,128)}, f32[180,256]{1,0:T(8,128)S(1)}, u32[]{:S(2)}, u32[]{:S(2)}) %collective-permute-start.5) | collective-permute-done | bytes 184352 | tf_op jit(solution)/shard_map/ppermute | solution.py:182
  42.8 0.0 copy-start.8
  42.8 0.0 collective-permute-done.4.even
  42.8 0.7 copy-done.8
  43.4 0.0 copy-start.9
  43.4 0.7 copy-done.9
  44.1 2.8 %second_product.1 = f32[8,128]{1,0:T(8,128)} custom-call(f32[5,5]{1,0:T(8,128)} %coup_ref.3, f32[5]{0:T(128)} %diff_ref.3, f32[5,16,256]{2,1,0:T(8,128)} %bitcast.45, f32[5,16,256]{2,1,0:T(8,128)} %bitcast.50, f32[3,16,256]{2,1,0:T(8,128)} %bitcast.56, f32[5,16,256]{2,1,0:T(8,128)} %bitcast.54, f32[29,256]{1,0:T(8,128)} %copy-done.7, f32[29,256]{1,0:T(8,128)} %copy-done.6, ...), custom_call_target="tpu_custom_call" | custom-call | tf_op jit(solution)/shard_map/second_product/pallas_call | solution.py:203
  46.9 14.1 %all_to_all.17 = f32[8,1,128]{2,1,0:T(1,128)S(1)} all-to-all(f32[8,1,128]{2,1,0:T(1,128)} %bitcast.59), channel_id=1, replica_groups=mesh['gx'=64,'gy'=8] {'gy'}, dimensions={0} | all-to-all | bytes 8192 | tf_op jit(solution)/shard_map/all_to_all | solution.py:211
  61.0 17.1 %all_to_all.18 = f32[64,1,128]{2,1,0:T(1,128)} all-to-all(f32[64,1,128]{2,1,0:T(1,128)S(1)} %broadcast_in_dim.2), channel_id=1, replica_groups=mesh['gx'=64,'gy'=8] {'gx'}, dimensions={0} | all-to-all | bytes 65536 | tf_op jit(solution)/shard_map/all_to_all | solution.py:213
  78.1 1.8 %combine.1 = (f32[5,16,256]{2,1,0:T(8,128)}, f32[5,16,256]{2,1,0:T(8,128)}) custom-call(f32[64,128]{1,0:T(8,128)} %bitcast.58, f32[5,16,256]{2,1,0:T(8,128)} %bitcast.46, f32[5,16,256]{2,1,0:T(8,128)} %bitcast.51, f32[180,256]{1,0:T(8,128)} %first_product.1.own), custom_call_target="tpu_custom_call" | custom-call | tf_op jit(solution)/shard_map/combine/pallas_call | solution.py:214
  (14 shorter events, 0.1 us)
Async XLA Ops:
  1.4 0.9 %copy-start.5 = (f32[3,1,16,256]{3,2,1,0:T(8,128)S(1)}, f32[3,1,16,256]{3,2,1,0:T(8,128)}, u32[]{:S(2)}) copy-start(f32[3,1,16,256]{3,2,1,0:T(8,128)} %param.8) | copy-start | bytes 147460
  2.3 0.9 %copy-start.4 = (f32[5,1,16,256]{3,2,1,0:T(8,128)S(1)}, f32[5,1,16,256]{3,2,1,0:T(8,128)}, u32[]{:S(2)}) copy-start(f32[5,1,16,256]{3,2,1,0:T(8,128)} %param.9) | copy-start | bytes 245764
  3.5 7.7 %collective-permute-start.1 = (f32[29,256]{1,0:T(8,128)S(1)}, f32[29,256]{1,0:T(8,128)S(1)}, u32[]{:S(2)}, u32[]{:S(2)}) collective-permute-start(f32[29,256]{1,0:T(8,128)S(1)} %concatenate.10), channel_id=1, source_target_pairs={{1,0},{2,1},{3,2},{4,3},{5,4},{6,5},{7,6},{0,7},{9,8},{10,9},{11,1... | collective-permute-start | bytes 89096 | tf_op jit(solution)/shard_map/ppermute | solution.py:176
  10.4 1.5 %copy-start = (f32[5,1,16,256]{3,2,1,0:T(8,128)S(1)}, f32[5,1,16,256]{3,2,1,0:T(8,128)}, u32[]{:S(2)}) copy-start(f32[5,1,16,256]{3,2,1,0:T(8,128)} %param.6) | copy-start | bytes 245764
  10.4 1.5 %copy-start.1 = (f32[5,1,16,256]{3,2,1,0:T(8,128)S(1)}, f32[5,1,16,256]{3,2,1,0:T(8,128)}, u32[]{:S(2)}) copy-start(f32[5,1,16,256]{3,2,1,0:T(8,128)} %param.7) | copy-start | bytes 245764
  10.7 1.2 %collective-permute-start = (f32[29,256]{1,0:T(8,128)S(1)}, f32[29,256]{1,0:T(8,128)S(1)}, u32[]{:S(2)}, u32[]{:S(2)}) collective-permute-start(f32[29,256]{1,0:T(8,128)S(1)} %concatenate.9), channel_id=1, source_target_pairs={{0,1},{1,2},{2,3},{3,4},{4,5},{5,6},{6,7},{7,0},{8,9},{9,10},{10,1... | collective-permute-start | bytes 89096 | tf_op jit(solution)/shard_map/ppermute | solution.py:175
  11.2 0.7 copy-start.6
  11.9 0.6 copy-start.7
  12.5 13.3 %collective-permute-start.3 = (f32[218,256]{1,0:T(8,128)S(1)}, f32[218,256]{1,0:T(8,128)S(1)}, u32[]{:S(2)}, u32[]{:S(2)}) collective-permute-start(f32[218,256]{1,0:T(8,128)S(1)} %concatenate.11), channel_id=1, source_target_pairs={{0,504},{8,16},{16,8},{24,32},{32,24},{40,48},{48,40},{56,64},{64,... | collective-permute-start | bytes 669704 | tf_op jit(solution)/shard_map/ppermute | solution.py:182
  22.4 7.1 %collective-permute-start.2 = (f32[218,256]{1,0:T(8,128)S(1)}, f32[218,256]{1,0:T(8,128)S(1)}, u32[]{:S(2)}, u32[]{:S(2)}) collective-permute-start(f32[218,256]{1,0:T(8,128)S(1)} %concatenate.11), channel_id=1, source_target_pairs={{0,8},{8,0},{16,24},{24,16},{32,40},{40,32},{48,56},{56,48},{64,72... | collective-permute-start | bytes 669704 | tf_op jit(solution)/shard_map/ppermute | solution.py:182
  25.8 3.7 %copy-start.2 = (f32[218,256]{1,0:T(8,128)}, f32[218,256]{1,0:T(8,128)S(1)}, u32[]{:S(2)}) copy-start(f32[218,256]{1,0:T(8,128)S(1)} %collective-permute-done.3.odd.odd1) | copy-start | bytes 669700
  29.5 0.7 copy-start.3
  32.9 9.8 %collective-permute-start.5 = (f32[180,256]{1,0:T(8,128)}, f32[180,256]{1,0:T(8,128)S(1)}, u32[]{:S(2)}, u32[]{:S(2)}) collective-permute-start(f32[180,256]{1,0:T(8,128)} %first_product.1.own), channel_id=1, source_target_pairs={{0,504},{8,16},{16,8},{24,32},{32,24},{40,48},{48,40},{56,64},{64,... | collective-permute-start | bytes 552968 | tf_op jit(solution)/shard_map/ppermute | solution.py:182
  36.0 6.8 %collective-permute-start.4 = (f32[180,256]{1,0:T(8,128)}, f32[180,256]{1,0:T(8,128)S(1)}, u32[]{:S(2)}, u32[]{:S(2)}) collective-permute-start(f32[180,256]{1,0:T(8,128)} %first_product.1.own), channel_id=1, source_target_pairs={{0,8},{8,0},{16,24},{24,16},{32,40},{40,32},{48,56},{56,48},{64,72... | collective-permute-start | bytes 552968 | tf_op jit(solution)/shard_map/ppermute | solution.py:182
  42.8 0.7 copy-start.8
  43.4 0.7 copy-start.9

commit v2 on v1

v2 whole, which is shorter than its diff:
```python
import functools

import jax
import jax.numpy as jnp
from jax import lax
from jax.experimental import pallas as pl
from jax.experimental.pallas import tpu as pltpu
from jax.sharding import PartitionSpec as P

CENTER = 8.0 / 3.0
EDGE = -1.0 / 6.0

COMPS = 5
FIELDS = 2 * COMPS
SUMS = 5


def up(v):
    size = v.shape[-1]
    lane = lax.broadcasted_iota(jnp.int32, v.shape, v.ndim - 1)
    return jnp.where(lane == size - 1, 0.0, pltpu.roll(v, size - 1, v.ndim - 1))


def down(v):
    lane = lax.broadcasted_iota(jnp.int32, v.shape, v.ndim - 1)
    return jnp.where(lane == 0, 0.0, pltpu.roll(v, 1, v.ndim - 1))


def apply_both(mid, even, odd, sign, vx, vy3, vz, vx_even, vx_odd, react, diff_ref, coup_ref):
    outs = []
    centers = [mid(f, 0) for f in range(FIELDS)]
    for f in range(FIELDS):
        c = f % COMPS
        right = f < COMPS
        b1, b0, b2 = centers[f], mid(f, -1), mid(f, 1)
        e1, o1 = even(f, 0), odd(f, 0)
        ya = (even(f, -1) + odd(f, -1)) + (even(f, 1) + odd(f, 1))
        t = (e1 + o1) + (b0 + b2) + 0.5 * ya
        d = diff_ref[c]
        base = (CENTER * d + react(c)) * b1
        if right:
            drift = (sign * vx) * (e1 - o1) + vy3[1] * (b2 - b0) + vz * (up(b1) - down(b1))
            out = base + (EDGE * d) * (ya + up(t) + down(t)) + 0.5 * drift
            for k in range(COMPS):
                out = out + coup_ref[c, k] * centers[k]
        else:
            fz = 0.5 * (vz * b1)
            g = (EDGE * d) * t
            drift = sign * (vx_even * e1 - vx_odd * o1) + (vy3[2] * b2 - vy3[0] * b0)
            out = base + (EDGE * d) * ya - 0.5 * drift + up(g - fz) + down(g + fz)
            for k in range(COMPS):
                out = out + coup_ref[k, c] * centers[COMPS + k]
        outs.append(out)
    return outs


def in_vmem(*arrays):
    return [pltpu.with_memory_space_constraint(v, pltpu.VMEM) for v in arrays]


def in_hbm(*arrays):
    return [pltpu.with_memory_space_constraint(v, pltpu.HBM) for v in arrays]


def in_smem(*arrays):
    return [pltpu.with_memory_space_constraint(v, pltpu.SMEM) for v in arrays]


def sign_here():
    return jnp.where(lax.rem(lax.axis_index("gx"), 2) == 0, 1.0, -1.0).astype(jnp.float32)


def load_kernel(ny, sr, sl, vel, rea, base, coef, low, high, sems):
    half = COMPS * ny
    copies = [
        pltpu.make_async_copy(src, dst, sems.at[k])
        for k, (src, dst) in enumerate(
            (
                (sr, base.at[0:half]),
                (sl, base.at[half : 2 * half]),
                (vel.at[0:ny], base.at[2 * half : 2 * half + ny]),
                (rea, coef.at[0:half]),
                (vel.at[ny : 3 * ny], coef.at[half : half + 2 * ny]),
            )
        )
    ]
    for copy in copies:
        copy.start()
    for copy in copies:
        copy.wait()
    for out, two, one in ((low, 0, 0), (high, ny - 2, ny - 1)):
        for f in range(FIELDS):
            out[2 * f : 2 * f + 2] = base[f * ny + two : f * ny + two + 2]
        row = 2 * FIELDS
        for c in range(COMPS):
            out[row + c : row + c + 1] = coef[c * ny + one : c * ny + one + 1]
        row += COMPS
        at = half + ny + one
        out[row : row + 1] = coef[at : at + 1]
        at = half + two
        out[row + 1 : row + 3] = coef[at : at + 2]
        at = 2 * half + one
        out[row + 3 : row + 4] = base[at : at + 1]


def fill_kernel(ny, base_in, coef_in, lo, hi, base, coef):
    del base_in, coef_in
    wide, thin = 2 * FIELDS, COMPS + 3
    at, last = (FIELDS + 1) * ny, (FIELDS + 1) * ny + 2 * wide
    base[at : at + wide] = lo[0:wide]
    base[at + wide : last] = hi[0:wide]
    base[last : last + 1] = lo[wide + thin : wide + thin + 1]
    base[last + 1 : last + 2] = hi[wide + thin : wide + thin + 1]
    at = (COMPS + 2) * ny
    coef[at : at + thin] = lo[wide : wide + thin]
    coef[at + thin : at + 2 * thin] = hi[wide : wide + thin]


def first_kernel(ny, coup_ref, diff_ref, base, coef, even, odd, out, field, cext):
    rows = ny + 8
    for f in range(FIELDS):
        for side, ref in ((0, base), (1, even), (2, odd)):
            field[side, f, 2 : ny + 2] = ref[f * ny : (f + 1) * ny]
            at = (FIELDS + 1) * ny + 2 * f
            field[side, f, 0:2] = ref[at : at + 2]
            at = at + 2 * FIELDS
            field[side, f, ny + 2 : ny + 4] = ref[at : at + 2]
    lo, hi = (COMPS + 2) * ny, (COMPS + 2) * ny + COMPS + 3
    for c in range(COMPS + 1):
        at = c * ny if c < COMPS else (COMPS + 1) * ny
        cext[c, 1 : ny + 1] = coef[at : at + ny]
        cext[c, 0:1] = coef[lo + c : lo + c + 1]
        cext[c, ny + 1 : ny + 2] = coef[hi + c : hi + c + 1]
    at, last = FIELDS * ny, (FIELDS + 1) * ny + 4 * FIELDS
    for k, ref in ((6, base), (7, even), (8, odd)):
        cext[k, 1 : ny + 1] = ref[at : at + ny]
        cext[k, 0:1] = ref[last : last + 1]
        cext[k, ny + 1 : ny + 2] = ref[last + 1 : last + 2]
    cext[9, 2 : ny + 2] = coef[COMPS * ny : (COMPS + 1) * ny]
    cext[9, 0:2] = coef[lo + COMPS + 1 : lo + COMPS + 3]
    cext[9, ny + 2 : ny + 4] = coef[hi + COMPS + 1 : hi + COMPS + 3]

    def plane(side):
        return lambda f, shift: field[side, f, 1 + shift : 1 + shift + rows]

    outs = apply_both(
        plane(0), plane(1), plane(2), sign_here(),
        cext[6, 0:rows], [cext[9, k : k + rows] for k in range(3)], cext[5, 0:rows],
        cext[7, 0:rows], cext[8, 0:rows], lambda c: cext[c, 0:rows], diff_ref, coup_ref,
    )
    for f in range(FIELDS):
        field[0, f, 0:rows] = outs[f]
        out[f * ny : (f + 1) * ny] = field[0, f, 1 : ny + 1]
        at = FIELDS * ny + 2 * f
        out[at : at + 1] = field[0, f, 0:1]
        out[at + 1 : at + 2] = field[0, f, ny + 1 : ny + 2]


def second_kernel(ny, copies, coup_ref, diff_ref, base, coef, even1, odd1, own, even, odd, out, field, vys):
    for f in range(FIELDS):
        for side, ref in ((0, own), (1, even), (2, odd)):
            field[side, f, 1 : ny + 1] = ref[f * ny : (f + 1) * ny]
            at = FIELDS * ny + 2 * f
            field[side, f, 0:1] = ref[at : at + 1]
            field[side, f, ny + 1 : ny + 2] = ref[at + 1 : at + 2]
    row = (COMPS + 2) * ny + COMPS + 2
    vys[1 : ny + 1] = coef[COMPS * ny : (COMPS + 1) * ny]
    vys[0:1] = coef[row : row + 1]
    row += COMPS + 2
    vys[ny + 1 : ny + 2] = coef[row : row + 1]

    def plane(side):
        return lambda f, shift: field[side, f, 1 + shift : 1 + shift + ny]

    at, vz = FIELDS * ny, (COMPS + 1) * ny
    outs = apply_both(
        plane(0), plane(1), plane(2), sign_here(),
        base[at : at + ny], [vys[k : k + ny] for k in range(3)], coef[vz : vz + ny],
        even1[at : at + ny], odd1[at : at + ny], lambda c: coef[c * ny : (c + 1) * ny], diff_ref, coup_ref,
    )
    lane = lax.broadcasted_iota(jnp.int32, (1, 128), 1)
    total = jnp.zeros((1, 128), jnp.float32)
    for system in range(2):
        sums = [0.0] * SUMS
        for f in range(system * COMPS, (system + 1) * COMPS):
            s, w1, w2 = base[f * ny : (f + 1) * ny], field[0, f, 1 : ny + 1], outs[f]
            for k, term in enumerate((w1 * w1, w1 * w2, w2 * w2, w1 * s, w2 * s)):
                sums[k] = sums[k] + term
        for k in range(SUMS):
            value = jnp.sum(jnp.sum(sums[k], axis=0, keepdims=True), axis=1, keepdims=True)
            total = total + jnp.where(lane == system * SUMS + k, value, 0.0)
    out[...] = jnp.broadcast_to(total, (copies, 128))


def last_kernel(ny, parts, base, own, out_r, out_l):
    total = jnp.sum(parts[...], axis=0, keepdims=True)
    lane = lax.broadcasted_iota(jnp.int32, (1, 128), 1)
    for system, out in ((0, out_r), (1, out_l)):
        g11, g12, g22, r1, r2 = [
            jnp.sum(jnp.where(lane == system * SUMS + k, total, 0.0), axis=1, keepdims=True)
            for k in range(SUMS)
        ]
        factor = g12 / g11
        b = (r2 - factor * r1) / (g22 - factor * g12)
        a = (r1 - g12 * b) / g11
        at = system * COMPS * ny
        out[...] = a * base[at : at + COMPS * ny] + b * own[at : at + COMPS * ny]


def per_device(right_border, left_border, velocity, reaction, diffusivity, coupling):
    comps, _, ny, nz = right_border.shape
    nx_count, ny_count = lax.axis_size("gx"), lax.axis_size("gy")
    f32 = jnp.float32
    params = pltpu.CompilerParams(vmem_limit_bytes=16 * 1024 * 1024)
    smem, vmem = pl.BlockSpec(memory_space=pltpu.SMEM), pl.BlockSpec(memory_space=pltpu.VMEM)
    sr, sl, vel, rea = (v.reshape(-1, nz) for v in (right_border, left_border, velocity, reaction))

    base_rows, coef_rows = (FIELDS + 1) * ny + 4 * FIELDS + 2, (COMPS + 2) * ny + 2 * (COMPS + 3)
    edge_rows = 2 * FIELDS + COMPS + 4
    base, coef, low, high = pl.pallas_call(
        functools.partial(load_kernel, ny),
        out_shape=[pltpu.VMEM((rows, nz), f32) for rows in (base_rows, coef_rows, edge_rows, edge_rows)],
        in_specs=[pl.BlockSpec(memory_space=pltpu.HBM)] * 4,
        out_specs=[vmem] * 4,
        scratch_shapes=[pltpu.SemaphoreType.DMA((5,))],
        compiler_params=params,
        name="load",
    )(*in_hbm(sr, sl, vel, rea))

    ahead = [(i, (i + 1) % ny_count) for i in range(ny_count)]
    back = [(j, i) for i, j in ahead]
    lo = lax.ppermute(high, "gy", ahead)
    hi = lax.ppermute(low, "gy", back)
    base, coef = pl.pallas_call(
        functools.partial(fill_kernel, ny),
        out_shape=[pltpu.VMEM(base.shape, f32), pltpu.VMEM(coef.shape, f32)],
        in_specs=[vmem] * 4,
        out_specs=[vmem] * 2,
        input_output_aliases={0: 0, 1: 1},
        compiler_params=params,
        name="fill",
    )(*in_vmem(base, coef, lo, hi))

    even_pairs = [(i, i ^ 1) for i in range(nx_count)]
    odd_pairs = [(i, (i - 1 if i % 2 == 0 else i + 1) % nx_count) for i in range(nx_count)]

    def swap(v):
        odd = lax.ppermute(v, "gx", odd_pairs)
        return lax.ppermute(v, "gx", even_pairs), odd

    even1, odd1 = swap(base)
    scalars = in_smem(coupling, diffusivity)
    own = pl.pallas_call(
        functools.partial(first_kernel, ny),
        out_shape=pltpu.VMEM((FIELDS * (ny + 2), nz), f32),
        in_specs=[smem] * 2 + [vmem] * 4,
        out_specs=vmem,
        scratch_shapes=[pltpu.VMEM((3, FIELDS, ny + 16, nz), f32), pltpu.VMEM((10, ny + 16, nz), f32)],
        compiler_params=params,
        name="first_product",
    )(*scalars, *in_vmem(base, coef, even1, odd1))
    even2, odd2 = swap(own)
    shares = pl.pallas_call(
        functools.partial(second_kernel, ny, ny_count),
        out_shape=pltpu.VMEM((ny_count, 128), f32),
        in_specs=[smem] * 2 + [vmem] * 7,
        out_specs=vmem,
        scratch_shapes=[pltpu.VMEM((3, FIELDS, ny + 8, nz), f32), pltpu.VMEM((ny + 8, nz), f32)],
        compiler_params=params,
        name="second_product",
    )(*scalars, *in_vmem(base, coef, even1, odd1, own, even2, odd2))
    shares = lax.all_to_all(shares, "gy", 0, 0, tiled=True)
    shares = jnp.broadcast_to(jnp.sum(shares, axis=0, keepdims=True), (nx_count, 128))
    shares = lax.all_to_all(shares, "gx", 0, 0, tiled=True)
    right, left = pl.pallas_call(
        functools.partial(last_kernel, ny),
        out_shape=[jax.ShapeDtypeStruct((comps * ny, nz), f32)] * 2,
        in_specs=[vmem] * 3,
        out_specs=[vmem] * 2,
        compiler_params=params,
        name="combine",
    )(*in_vmem(shares, base, own))
    return right.reshape(right_border.shape), left.reshape(left_border.shape)


def solution(mesh):
    block = P(None, "gx", "gy", None)
    return jax.shard_map(
        per_device,
        mesh=mesh,
        in_specs=(block, block, block, block, P(), P()),
        out_specs=(block, block),
        check_vma=False,
    )
```

time: 80.4 us -> 72.9 us (0.907)
  local copies, waits for them, and re-layouts: 5.72 us -> 0.03 us
  blocking collectives: 31.2 us -> 28.4 us
  Pallas kernels: 7.35 us -> 4.68 us
  starting transfers between devices: 23.7 us -> 26.1 us
  waiting for transfers between devices: 11.1 us -> 12.5 us
    unnamed x21 -> x4, local copies, waits for them, and re-layouts: 3.32 us -> 0.01 us
    all_to_all x1, blocking collectives: 14.1 us -> 10.9 us  [per_device(): shares = lax.all_to_all(shares, 'gy', 0, 0, tiled=True)]
    ppermute x6, starting transfers between devices: 23.7 us -> 26.1 us  [the longest x2 15.4 us: swap(): odd = lax.ppermute(v, 'gx', odd_pairs)]
    slice x6 -> x0, local copies, waits for them, and re-layouts: 1.63 us -> none  [the longest x2 1.62 us: edge(): pick = lambda v, where: v[..., where, :].reshape(-1, nz)]
    pallas_call x1, Pallas kernels: 2.77 us -> 1.36 us  [per_device(): pl.pallas_call(functools.partial(second_kernel, ny, ny_count), out_shape=...]
    ppermute x6, waiting for transfers between devices: 11.1 us -> 12.5 us  [the longest x2 8.51 us: swap(): odd = lax.ppermute(v, 'gx', odd_pairs)]
    pallas_call x1, Pallas kernels: 1.8 us -> 0.78 us  [per_device(): pl.pallas_call(functools.partial(last_kernel, ny), out_shape=[jax.ShapeDt...]
    pallas_call x1 -> x3, Pallas kernels: 2.78 us -> 2.54 us  [the longest x1 1.47 us: per_device(): pl.pallas_call(functools.partial(first_kernel, ny), out_shape=pltpu.VMEM(...]
  transfers between devices with their start and end apart: 6 -> 6, of which waited for: 5 -> 6; matrix products, arithmetic and copies ran while one was open for 0% -> 0% of each run, Pallas kernels for 0% -> 0%
where the time goes in v2:
time: 72.9 us; the launch traced here: 72.5 us
  blocking collectives  28.4 us (39%)
  starting transfers between devices  26.1 us (36%)
  waiting for transfers between devices  12.5 us (17%)
  Pallas kernels  4.68 us (6%)
    all_to_all x1, blocking collectives, per_device(): shares = lax.all_to_all(shares, 'gx', 0, 0, tiled=True)  17.5 us
    ppermute x2, starting transfers between devices, swap(): odd = lax.ppermute(v, 'gx', odd_pairs)  15.4 us
    all_to_all x1, blocking collectives, per_device(): shares = lax.all_to_all(shares, 'gy', 0, 0, tiled=True)  10.9 us
    ppermute x2, waiting for transfers between devices, swap(): odd = lax.ppermute(v, 'gx', odd_pairs)  8.51 us
    ppermute x1, starting transfers between devices, per_device(): hi = lax.ppermute(low, 'gy', back)  4.3 us
    ppermute x2, starting transfers between devices, swap(): return (lax.ppermute(v, 'gx', even_pairs), odd)  3.84 us
    ppermute x2, waiting for transfers between devices, swap(): return (lax.ppermute(v, 'gx', even_pairs), odd)  3.16 us
    ppermute x1, starting transfers between devices, per_device(): lo = lax.ppermute(high, 'gy', ahead)  2.61 us
  transfers between devices with their start and end apart: 6, of which 6 were waited for; matrix products, arithmetic and copies ran while one was open for 0% of the time, Pallas kernels for 0%

profile of v2, /device:TPU:1, one launch (start us, length us, event | category | flops | bytes accessed | tf_op | source)
XLA Modules:
  0.0 72.5 jit_solution(5263170127958052062)
XLA Ops:
  0.6 1.1 %load.1 = (f32[218,256]{1,0:T(8,128)S(1)}, f32[128,256]{1,0:T(8,128)S(1)}, f32[29,256]{1,0:T(8,128)S(1)}, f32[29,256]{1,0:T(8,128)S(1)}) custom-call(f32[80,256]{1,0:T(8,128)} %bitcast.16, f32[80,256]{1,0:T(8,128)} %bitcast.17, f32[48,256]{1,0:T(8,128)} %bitcast.19, f32[80,256]{1,0:T(8,128)} %bitcast.18), custom_call_target="tpu_custom_call" | custom-call | tf_op jit(solution)/shard_map/load/pallas_call | solution.py:220
  1.7 2.6 %collective-permute-start = (f32[29,256]{1,0:T(8,128)S(1)}, f32[29,256]{1,0:T(8,128)S(1)}, u32[]{:S(2)}, u32[]{:S(2)}) collective-permute-start(f32[29,256]{1,0:T(8,128)S(1)} %get-tuple-element.12), channel_id=1, source_target_pairs={{0,1},{1,2},{2,3},{3,4},{4,5},{5,6},{6,7},{7,0},{8,9},{9,10},{10,1... | collective-permute-start | bytes 89096 | tf_op jit(solution)/shard_map/ppermute | solution.py:232
  4.3 4.3 %collective-permute-start.1 = (f32[29,256]{1,0:T(8,128)S(1)}, f32[29,256]{1,0:T(8,128)S(1)}, u32[]{:S(2)}, u32[]{:S(2)}) collective-permute-start(f32[29,256]{1,0:T(8,128)S(1)} %get-tuple-element.13), channel_id=1, source_target_pairs={{1,0},{2,1},{3,2},{4,3},{5,4},{6,5},{7,6},{0,7},{9,8},{10,9},{11,1... | collective-permute-start | bytes 89096 | tf_op jit(solution)/shard_map/ppermute | solution.py:233
  8.6 0.7 collective-permute-done.lo
  9.3 0.2 collective-permute-done.1.hi
  9.5 0.0 copy-start
  9.5 0.0 copy-start.1
  9.5 11.8 %collective-permute-start.3 = (f32[218,256]{1,0:T(8,128)S(1)}, f32[218,256]{1,0:T(8,128)S(1)}, u32[]{:S(2)}, u32[]{:S(2)}) collective-permute-start(f32[218,256]{1,0:T(8,128)S(1)} %get-tuple-element.14.base), channel_id=1, source_target_pairs={{0,504},{8,16},{16,8},{24,32},{32,24},{40,48},{48,40},{56,64},{64,... | collective-permute-start | bytes 669704 | tf_op jit(solution)/shard_map/ppermute | solution.py:248
  21.3 1.9 %collective-permute-start.2 = (f32[218,256]{1,0:T(8,128)S(1)}, f32[218,256]{1,0:T(8,128)S(1)}, u32[]{:S(2)}, u32[]{:S(2)}) collective-permute-start(f32[218,256]{1,0:T(8,128)S(1)} %get-tuple-element.14.base), channel_id=1, source_target_pairs={{0,8},{8,0},{16,24},{24,16},{32,40},{40,32},{48,56},{56,48},{64,72... | collective-permute-start | bytes 669704 | tf_op jit(solution)/shard_map/ppermute | solution.py:249
  23.2 3.9 %collective-permute-done.3.odd.odd1 = f32[218,256]{1,0:T(8,128)S(1)} collective-permute-done((f32[218,256]{1,0:T(8,128)S(1)}, f32[218,256]{1,0:T(8,128)S(1)}, u32[]{:S(2)}, u32[]{:S(2)}) %collective-permute-start.3) | collective-permute-done | bytes 223264 | tf_op jit(solution)/shard_map/ppermute | solution.py:248
  27.1 2.8 %collective-permute-done.2.even.even1 = f32[218,256]{1,0:T(8,128)S(1)} collective-permute-done((f32[218,256]{1,0:T(8,128)S(1)}, f32[218,256]{1,0:T(8,128)S(1)}, u32[]{:S(2)}, u32[]{:S(2)}) %collective-permute-start.2) | collective-permute-done | bytes 223264 | tf_op jit(solution)/shard_map/ppermute | solution.py:249
  29.9 0.0 copy-done
  29.9 0.0 copy-done.1
  29.9 1.5 %first_product.1.own = f32[180,256]{1,0:T(8,128)S(1)} custom-call(f32[5,5]{1,0:T(8,128)S(1)} %copy-done, f32[5]{0:T(128)S(1)} %copy-done.1, f32[218,256]{1,0:T(8,128)S(1)} %get-tuple-element.14.base, f32[128,256]{1,0:T(8,128)S(1)} %get-tuple-element.15.coef, f32[218,256]{1,0:T(8,128)S(1)} %collective-permute-done.2.even.even1, ...), custom_call_target="tpu_custom_call" | custom-call | tf_op jit(solution)/shard_map/first_product/pallas_call | solution.py:253
  31.4 3.6 %collective-permute-start.5 = (f32[180,256]{1,0:T(8,128)S(1)}, f32[180,256]{1,0:T(8,128)S(1)}, u32[]{:S(2)}, u32[]{:S(2)}) collective-permute-start(f32[180,256]{1,0:T(8,128)S(1)} %first_product.1.own), channel_id=1, source_target_pairs={{0,504},{8,16},{16,8},{24,32},{32,24},{40,48},{48,40},{56,64},{64,... | collective-permute-start | bytes 552968 | tf_op jit(solution)/shard_map/ppermute | solution.py:248
  35.0 1.9 %collective-permute-start.4 = (f32[180,256]{1,0:T(8,128)S(1)}, f32[180,256]{1,0:T(8,128)S(1)}, u32[]{:S(2)}, u32[]{:S(2)}) collective-permute-start(f32[180,256]{1,0:T(8,128)S(1)} %first_product.1.own), channel_id=1, source_target_pairs={{0,8},{8,0},{16,24},{24,16},{32,40},{40,32},{48,56},{56,48},{64,72... | collective-permute-start | bytes 552968 | tf_op jit(solution)/shard_map/ppermute | solution.py:249
  37.0 4.6 %collective-permute-done.5.odd = f32[180,256]{1,0:T(8,128)S(1)} collective-permute-done((f32[180,256]{1,0:T(8,128)S(1)}, f32[180,256]{1,0:T(8,128)S(1)}, u32[]{:S(2)}, u32[]{:S(2)}) %collective-permute-start.5) | collective-permute-done | bytes 184352 | tf_op jit(solution)/shard_map/ppermute | solution.py:248
  41.6 0.4 collective-permute-done.4.even
  41.9 1.4 %second_product.1 = f32[8,128]{1,0:T(8,128)S(1)} custom-call(f32[5,5]{1,0:T(8,128)S(1)} %copy-done, f32[5]{0:T(128)S(1)} %copy-done.1, f32[218,256]{1,0:T(8,128)S(1)} %get-tuple-element.14.base, f32[128,256]{1,0:T(8,128)S(1)} %get-tuple-element.15.coef, f32[218,256]{1,0:T(8,128)S(1)} %collective-permute-done.2.even.even1, ...), custom_call_target="tpu_custom_call" | custom-call | tf_op jit(solution)/shard_map/second_product/pallas_call | solution.py:263
  43.3 10.9 %all_to_all.17 = f32[8,1,128]{2,1,0:T(1,128)S(1)} all-to-all(f32[8,1,128]{2,1,0:T(1,128)S(1)} %bitcast.15), channel_id=1, replica_groups=mesh['gx'=64,'gy'=8] {'gy'}, dimensions={0} | all-to-all | bytes 8192 | tf_op jit(solution)/shard_map/all_to_all | solution.py:272
  54.3 17.5 %all_to_all.18 = f32[64,1,128]{2,1,0:T(1,128)S(1)} all-to-all(f32[64,1,128]{2,1,0:T(1,128)S(1)} %broadcast_in_dim.2), channel_id=1, replica_groups=mesh['gx'=64,'gy'=8] {'gx'}, dimensions={0} | all-to-all | bytes 65536 | tf_op jit(solution)/shard_map/all_to_all | solution.py:274
  71.7 0.8 %combine.1 = (f32[80,256]{1,0:T(8,128)}, f32[80,256]{1,0:T(8,128)}) custom-call(f32[64,128]{1,0:T(8,128)S(1)} %bitcast.14, f32[218,256]{1,0:T(8,128)S(1)} %get-tuple-element.14.base, f32[180,256]{1,0:T(8,128)S(1)} %first_product.1.own), custom_call_target="tpu_custom_call" | custom-call | tf_op jit(solution)/shard_map/combine/pallas_call | solution.py:275
  (3 shorter events, 0.1 us)
Async XLA Ops:
  1.7 7.6 %collective-permute-start = (f32[29,256]{1,0:T(8,128)S(1)}, f32[29,256]{1,0:T(8,128)S(1)}, u32[]{:S(2)}, u32[]{:S(2)}) collective-permute-start(f32[29,256]{1,0:T(8,128)S(1)} %get-tuple-element.12), channel_id=1, source_target_pairs={{0,1},{1,2},{2,3},{3,4},{4,5},{5,6},{6,7},{7,0},{8,9},{9,10},{10,1... | collective-permute-start | bytes 89096 | tf_op jit(solution)/shard_map/ppermute | solution.py:232
  4.3 5.2 %collective-permute-start.1 = (f32[29,256]{1,0:T(8,128)S(1)}, f32[29,256]{1,0:T(8,128)S(1)}, u32[]{:S(2)}, u32[]{:S(2)}) collective-permute-start(f32[29,256]{1,0:T(8,128)S(1)} %get-tuple-element.13), channel_id=1, source_target_pairs={{1,0},{2,1},{3,2},{4,3},{5,4},{6,5},{7,6},{0,7},{9,8},{10,9},{11,1... | collective-permute-start | bytes 89096 | tf_op jit(solution)/shard_map/ppermute | solution.py:233
  9.5 20.4 %copy-start = (f32[5,5]{1,0:T(8,128)S(1)}, f32[5,5]{1,0:T(8,128)}, u32[]{:S(2)}) copy-start(f32[5,5]{1,0:T(8,128)} %coup_ref.3) | copy-start | bytes 304
  9.5 20.4 %copy-start.1 = (f32[5]{0:T(128)S(1)}, f32[5]{0:T(128)}, u32[]{:S(2)}) copy-start(f32[5]{0:T(128)} %diff_ref.3) | copy-start | bytes 64
  9.5 17.6 %collective-permute-start.3 = (f32[218,256]{1,0:T(8,128)S(1)}, f32[218,256]{1,0:T(8,128)S(1)}, u32[]{:S(2)}, u32[]{:S(2)}) collective-permute-start(f32[218,256]{1,0:T(8,128)S(1)} %get-tuple-element.14.base), channel_id=1, source_target_pairs={{0,504},{8,16},{16,8},{24,32},{32,24},{40,48},{48,40},{56,64},{64,... | collective-permute-start | bytes 669704 | tf_op jit(solution)/shard_map/ppermute | solution.py:248
  21.3 8.6 %collective-permute-start.2 = (f32[218,256]{1,0:T(8,128)S(1)}, f32[218,256]{1,0:T(8,128)S(1)}, u32[]{:S(2)}, u32[]{:S(2)}) collective-permute-start(f32[218,256]{1,0:T(8,128)S(1)} %get-tuple-element.14.base), channel_id=1, source_target_pairs={{0,8},{8,0},{16,24},{24,16},{32,40},{40,32},{48,56},{56,48},{64,72... | collective-permute-start | bytes 669704 | tf_op jit(solution)/shard_map/ppermute | solution.py:249
  31.4 10.2 %collective-permute-start.5 = (f32[180,256]{1,0:T(8,128)S(1)}, f32[180,256]{1,0:T(8,128)S(1)}, u32[]{:S(2)}, u32[]{:S(2)}) collective-permute-start(f32[180,256]{1,0:T(8,128)S(1)} %first_product.1.own), channel_id=1, source_target_pairs={{0,504},{8,16},{16,8},{24,32},{32,24},{40,48},{48,40},{56,64},{64,... | collective-permute-start | bytes 552968 | tf_op jit(solution)/shard_map/ppermute | solution.py:248
  35.0 6.9 %collective-permute-start.4 = (f32[180,256]{1,0:T(8,128)S(1)}, f32[180,256]{1,0:T(8,128)S(1)}, u32[]{:S(2)}, u32[]{:S(2)}) collective-permute-start(f32[180,256]{1,0:T(8,128)S(1)} %first_product.1.own), channel_id=1, source_target_pairs={{0,8},{8,0},{16,24},{24,16},{32,40},{40,32},{48,56},{56,48},{64,72... | collective-permute-start | bytes 552968 | tf_op jit(solution)/shard_map/ppermute | solution.py:249

commit v3 on v2

--- a/solution.py
+++ b/solution.py
@@ -26,7 +26,9 @@
     return jnp.where(lane == 0, 0.0, pltpu.roll(v, 1, v.ndim - 1))
 
 
-def apply_both(mid, even, odd, sign, vx, vy3, vz, vx_even, vx_odd, react, diff_ref, coup_ref):
+def apply_both(mid, even, odd, vx, vy3, vz, vx_even, vx_odd, react, scal):
+    number = lambda k: scal[k : k + 1]
+    sign = number(COMPS * COMPS + COMPS)
     outs = []
     centers = [mid(f, 0) for f in range(FIELDS)]
     for f in range(FIELDS):
@@ -36,20 +38,20 @@
         e1, o1 = even(f, 0), odd(f, 0)
         ya = (even(f, -1) + odd(f, -1)) + (even(f, 1) + odd(f, 1))
         t = (e1 + o1) + (b0 + b2) + 0.5 * ya
-        d = diff_ref[c]
+        d = number(COMPS * COMPS + c)
         base = (CENTER * d + react(c)) * b1
         if right:
             drift = (sign * vx) * (e1 - o1) + vy3[1] * (b2 - b0) + vz * (up(b1) - down(b1))
             out = base + (EDGE * d) * (ya + up(t) + down(t)) + 0.5 * drift
             for k in range(COMPS):
-                out = out + coup_ref[c, k] * centers[k]
+                out = out + number(c * COMPS + k) * centers[k]
         else:
             fz = 0.5 * (vz * b1)
             g = (EDGE * d) * t
             drift = sign * (vx_even * e1 - vx_odd * o1) + (vy3[2] * b2 - vy3[0] * b0)
             out = base + (EDGE * d) * ya - 0.5 * drift + up(g - fz) + down(g + fz)
             for k in range(COMPS):
-                out = out + coup_ref[k, c] * centers[COMPS + k]
+                out = out + number(k * COMPS + c) * centers[COMPS + k]
         outs.append(out)
     return outs
 
@@ -62,12 +64,14 @@
     return [pltpu.with_memory_space_constraint(v, pltpu.HBM) for v in arrays]
 
 
-def in_smem(*arrays):
-    return [pltpu.with_memory_space_constraint(v, pltpu.SMEM) for v in arrays]
-
-
-def sign_here():
-    return jnp.where(lax.rem(lax.axis_index("gx"), 2) == 0, 1.0, -1.0).astype(jnp.float32)
+def numbers_kernel(coup_ref, diff_ref, scal):
+    for k in range(COMPS * COMPS):
+        scal[k : k + 1] = jnp.full((1, scal.shape[1]), coup_ref[k // COMPS, k % COMPS], jnp.float32)
+    for c in range(COMPS):
+        scal[COMPS * COMPS + c : COMPS * COMPS + c + 1] = jnp.full((1, scal.shape[1]), diff_ref[c], jnp.float32)
+    sign = jnp.where(lax.rem(lax.axis_index("gx"), 2) == 0, 1.0, -1.0).astype(jnp.float32)
+    last = COMPS * COMPS + COMPS
+    scal[last : last + 1] = jnp.full((1, scal.shape[1]), sign, jnp.float32)
 
 
 def load_kernel(ny, sr, sl, vel, rea, base, coef, low, high, sems):
@@ -116,7 +120,7 @@
     coef[at + thin : at + 2 * thin] = hi[wide : wide + thin]
 
 
-def first_kernel(ny, coup_ref, diff_ref, base, coef, even, odd, out, field, cext):
+def first_kernel(ny, scal, base, coef, even, odd, out, field, cext):
     rows = ny + 8
     for f in range(FIELDS):
         for side, ref in ((0, base), (1, even), (2, odd)):
@@ -144,9 +148,9 @@
         return lambda f, shift: field[side, f, 1 + shift : 1 + shift + rows]
 
     outs = apply_both(
-        plane(0), plane(1), plane(2), sign_here(),
+        plane(0), plane(1), plane(2),
         cext[6, 0:rows], [cext[9, k : k + rows] for k in range(3)], cext[5, 0:rows],
-        cext[7, 0:rows], cext[8, 0:rows], lambda c: cext[c, 0:rows], diff_ref, coup_ref,
+        cext[7, 0:rows], cext[8, 0:rows], lambda c: cext[c, 0:rows], scal,
     )
     for f in range(FIELDS):
         field[0, f, 0:rows] = outs[f]
@@ -156,7 +160,7 @@
         out[at + 1 : at + 2] = field[0, f, ny + 1 : ny + 2]
 
 
-def second_kernel(ny, copies, coup_ref, diff_ref, base, coef, even1, odd1, own, even, odd, out, field, vys):
+def second_kernel(ny, copies, scal, base, coef, even1, odd1, own, even, odd, out, field, vys):
     for f in range(FIELDS):
         for side, ref in ((0, own), (1, even), (2, odd)):
             field[side, f, 1 : ny + 1] = ref[f * ny : (f + 1) * ny]
@@ -174,9 +178,9 @@
 
     at, vz = FIELDS * ny, (COMPS + 1) * ny
     outs = apply_both(
-        plane(0), plane(1), plane(2), sign_here(),
+        plane(0), plane(1), plane(2),
         base[at : at + ny], [vys[k : k + ny] for k in range(3)], coef[vz : vz + ny],
-        even1[at : at + ny], odd1[at : at + ny], lambda c: coef[c * ny : (c + 1) * ny], diff_ref, coup_ref,
+        even1[at : at + ny], odd1[at : at + ny], lambda c: coef[c * ny : (c + 1) * ny], scal,
     )
     lane = lax.broadcasted_iota(jnp.int32, (1, 128), 1)
     total = jnp.zeros((1, 128), jnp.float32)
@@ -227,6 +231,15 @@
         name="load",
     )(*in_hbm(sr, sl, vel, rea))
 
+    scal = pl.pallas_call(
+        numbers_kernel,
+        out_shape=pltpu.VMEM((32, nz), f32),
+        in_specs=[smem] * 2,
+        out_specs=vmem,
+        compiler_params=params,
+        name="numbers",
+    )(coupling, diffusivity)
+
     ahead = [(i, (i + 1) % ny_count) for i in range(ny_count)]
     back = [(j, i) for i, j in ahead]
     lo = lax.ppermute(high, "gy", ahead)
@@ -249,26 +262,25 @@
         return lax.ppermute(v, "gx", even_pairs), odd
 
     even1, odd1 = swap(base)
-    scalars = in_smem(coupling, diffusivity)
     own = pl.pallas_call(
         functools.partial(first_kernel, ny),
         out_shape=pltpu.VMEM((FIELDS * (ny + 2), nz), f32),
-        in_specs=[smem] * 2 + [vmem] * 4,
+        in_specs=[vmem] * 5,
         out_specs=vmem,
         scratch_shapes=[pltpu.VMEM((3, FIELDS, ny + 16, nz), f32), pltpu.VMEM((10, ny + 16, nz), f32)],
         compiler_params=params,
         name="first_product",
-    )(*scalars, *in_vmem(base, coef, even1, odd1))
+    )(*in_vmem(scal, base, coef, even1, odd1))
     even2, odd2 = swap(own)
     shares = pl.pallas_call(
         functools.partial(second_kernel, ny, ny_count),
         out_shape=pltpu.VMEM((ny_count, 128), f32),
-        in_specs=[smem] * 2 + [vmem] * 7,
+        in_specs=[vmem] * 8,
         out_specs=vmem,
         scratch_shapes=[pltpu.VMEM((3, FIELDS, ny + 8, nz), f32), pltpu.VMEM((ny + 8, nz), f32)],
         compiler_params=params,
         name="second_product",
-    )(*scalars, *in_vmem(base, coef, even1, odd1, own, even2, odd2))
+    )(*in_vmem(scal, base, coef, even1, odd1, own, even2, odd2))
     shares = lax.all_to_all(shares, "gy", 0, 0, tiled=True)
     shares = jnp.broadcast_to(jnp.sum(shares, axis=0, keepdims=True), (nx_count, 128))
     shares = lax.all_to_all(shares, "gx", 0, 0, tiled=True)

time: 72.9 us -> 71.6 us (0.982)
  transfers between devices with their start and end apart: 6 -> 6, of which waited for: 6 -> 6; matrix products, arithmetic and copies ran while one was open for 0% -> 0% of each run, Pallas kernels for 0% -> 1%
where the time goes in v3:
time: 71.6 us; the launch traced here: 71.3 us
  blocking collectives  28.4 us (40%)
  starting transfers between devices  26.1 us (36%)
  waiting for transfers between devices  11.9 us (17%)
  Pallas kernels  4.11 us (6%)
  between operations  0.72 us (1%)
    all_to_all x1, blocking collectives, per_device(): shares = lax.all_to_all(shares, 'gx', 0, 0, tiled=True)  17.5 us
    ppermute x2, starting transfers between devices, swap(): odd = lax.ppermute(v, 'gx', odd_pairs)  15.4 us
    all_to_all x1, blocking collectives, per_device(): shares = lax.all_to_all(shares, 'gy', 0, 0, tiled=True)  11 us
    ppermute x2, waiting for transfers between devices, swap(): odd = lax.ppermute(v, 'gx', odd_pairs)  7.86 us
    ppermute x1, starting transfers between devices, per_device(): hi = lax.ppermute(low, 'gy', back)  4.3 us
    ppermute x2, starting transfers between devices, swap(): return (lax.ppermute(v, 'gx', even_pairs), odd)  3.84 us
    ppermute x2, waiting for transfers between devices, swap(): return (lax.ppermute(v, 'gx', even_pairs), odd)  3.16 us
    ppermute x1, starting transfers between devices, per_device(): lo = lax.ppermute(high, 'gy', ahead)  2.61 us
  transfers between devices with their start and end apart: 6, of which 6 were waited for; matrix products, arithmetic and copies ran while one was open for 0% of the time, Pallas kernels for 1%

profile of v3, /device:TPU:1, one launch (start us, length us, event | category | flops | bytes accessed | tf_op | source)
XLA Modules:
  0.0 71.3 jit_solution(2170714372681995283)
XLA Ops:
  0.6 1.1 %load.1 = (f32[218,256]{1,0:T(8,128)S(1)}, f32[128,256]{1,0:T(8,128)S(1)}, f32[29,256]{1,0:T(8,128)S(1)}, f32[29,256]{1,0:T(8,128)S(1)}) custom-call(f32[80,256]{1,0:T(8,128)} %bitcast.16, f32[80,256]{1,0:T(8,128)} %bitcast.17, f32[48,256]{1,0:T(8,128)} %bitcast.19, f32[80,256]{1,0:T(8,128)} %bitcast.18), custom_call_target="tpu_custom_call" | custom-call | tf_op jit(solution)/shard_map/load/pallas_call | solution.py:224
  1.7 2.6 %collective-permute-start = (f32[29,256]{1,0:T(8,128)S(1)}, f32[29,256]{1,0:T(8,128)S(1)}, u32[]{:S(2)}, u32[]{:S(2)}) collective-permute-start(f32[29,256]{1,0:T(8,128)S(1)} %get-tuple-element.12), channel_id=1, source_target_pairs={{0,1},{1,2},{2,3},{3,4},{4,5},{5,6},{6,7},{7,0},{8,9},{9,10},{10,1... | collective-permute-start | bytes 89096 | tf_op jit(solution)/shard_map/ppermute | solution.py:245
  4.3 4.3 %collective-permute-start.1 = (f32[29,256]{1,0:T(8,128)S(1)}, f32[29,256]{1,0:T(8,128)S(1)}, u32[]{:S(2)}, u32[]{:S(2)}) collective-permute-start(f32[29,256]{1,0:T(8,128)S(1)} %get-tuple-element.13), channel_id=1, source_target_pairs={{1,0},{2,1},{3,2},{4,3},{5,4},{6,5},{7,6},{0,7},{9,8},{10,9},{11,1... | collective-permute-start | bytes 89096 | tf_op jit(solution)/shard_map/ppermute | solution.py:246
  8.6 0.7 collective-permute-done.lo
  9.3 0.2 collective-permute-done.1.hi
  9.5 0.0 copy-start
  9.5 0.0 copy-start.1
  9.5 11.8 %collective-permute-start.3 = (f32[218,256]{1,0:T(8,128)S(1)}, f32[218,256]{1,0:T(8,128)S(1)}, u32[]{:S(2)}, u32[]{:S(2)}) collective-permute-start(f32[218,256]{1,0:T(8,128)S(1)} %get-tuple-element.14.base), channel_id=1, source_target_pairs={{0,504},{8,16},{16,8},{24,32},{32,24},{40,48},{48,40},{56,64},{64,... | collective-permute-start | bytes 669704 | tf_op jit(solution)/shard_map/ppermute | solution.py:261
  21.3 1.9 %collective-permute-start.2 = (f32[218,256]{1,0:T(8,128)S(1)}, f32[218,256]{1,0:T(8,128)S(1)}, u32[]{:S(2)}, u32[]{:S(2)}) collective-permute-start(f32[218,256]{1,0:T(8,128)S(1)} %get-tuple-element.14.base), channel_id=1, source_target_pairs={{0,8},{8,0},{16,24},{24,16},{32,40},{40,32},{48,56},{56,48},{64,72... | collective-permute-start | bytes 669704 | tf_op jit(solution)/shard_map/ppermute | solution.py:262
  23.2 0.0 copy-done
  23.2 0.0 copy-done.1
  23.2 0.6 numbers.1.scal
  23.8 3.3 %collective-permute-done.3.odd.odd1 = f32[218,256]{1,0:T(8,128)S(1)} collective-permute-done((f32[218,256]{1,0:T(8,128)S(1)}, f32[218,256]{1,0:T(8,128)S(1)}, u32[]{:S(2)}, u32[]{:S(2)}) %collective-permute-start.3) | collective-permute-done | bytes 223264 | tf_op jit(solution)/shard_map/ppermute | solution.py:261
  27.1 2.8 %collective-permute-done.2.even.even1 = f32[218,256]{1,0:T(8,128)S(1)} collective-permute-done((f32[218,256]{1,0:T(8,128)S(1)}, f32[218,256]{1,0:T(8,128)S(1)}, u32[]{:S(2)}, u32[]{:S(2)}) %collective-permute-start.2) | collective-permute-done | bytes 223264 | tf_op jit(solution)/shard_map/ppermute | solution.py:262
  29.9 0.9 %first_product.1.own = f32[180,256]{1,0:T(8,128)S(1)} custom-call(f32[32,256]{1,0:T(8,128)S(1)} %numbers.1.scal, f32[218,256]{1,0:T(8,128)S(1)} %get-tuple-element.14.base, f32[128,256]{1,0:T(8,128)S(1)} %get-tuple-element.15.coef, f32[218,256]{1,0:T(8,128)S(1)} %collective-permute-done.2.even.even1, f32[218,256]{1,0:T(8,128)S(1)} %collective-permute-done.3.odd.odd1), custom_call_target="tpu_custom_call" | custom-call | tf_op jit(solution)/shard_map/first_product/pallas_call | solution.py:265
  30.8 3.6 %collective-permute-start.5 = (f32[180,256]{1,0:T(8,128)S(1)}, f32[180,256]{1,0:T(8,128)S(1)}, u32[]{:S(2)}, u32[]{:S(2)}) collective-permute-start(f32[180,256]{1,0:T(8,128)S(1)} %first_product.1.own), channel_id=1, source_target_pairs={{0,504},{8,16},{16,8},{24,32},{32,24},{40,48},{48,40},{56,64},{64,... | collective-permute-start | bytes 552968 | tf_op jit(solution)/shard_map/ppermute | solution.py:261
  34.4 1.9 %collective-permute-start.4 = (f32[180,256]{1,0:T(8,128)S(1)}, f32[180,256]{1,0:T(8,128)S(1)}, u32[]{:S(2)}, u32[]{:S(2)}) collective-permute-start(f32[180,256]{1,0:T(8,128)S(1)} %first_product.1.own), channel_id=1, source_target_pairs={{0,8},{8,0},{16,24},{24,16},{32,40},{40,32},{48,56},{56,48},{64,72... | collective-permute-start | bytes 552968 | tf_op jit(solution)/shard_map/ppermute | solution.py:262
  36.4 4.6 %collective-permute-done.5.odd = f32[180,256]{1,0:T(8,128)S(1)} collective-permute-done((f32[180,256]{1,0:T(8,128)S(1)}, f32[180,256]{1,0:T(8,128)S(1)}, u32[]{:S(2)}, u32[]{:S(2)}) %collective-permute-start.5) | collective-permute-done | bytes 184352 | tf_op jit(solution)/shard_map/ppermute | solution.py:261
  41.0 0.4 collective-permute-done.4.even
  41.3 0.8 %second_product.1 = f32[8,128]{1,0:T(8,128)S(1)} custom-call(f32[32,256]{1,0:T(8,128)S(1)} %numbers.1.scal, f32[218,256]{1,0:T(8,128)S(1)} %get-tuple-element.14.base, f32[128,256]{1,0:T(8,128)S(1)} %get-tuple-element.15.coef, f32[218,256]{1,0:T(8,128)S(1)} %collective-permute-done.2.even.even1, f32[218,256]{1,0:T(8,128)S(1)} %collective-permute-done.3.odd.odd1, ...), custom_call_target="tpu_custom_call" | custom-call | tf_op jit(solution)/shard_map/second_product/pallas_call | solution.py:275
  42.1 11.0 %all_to_all.17 = f32[8,1,128]{2,1,0:T(1,128)S(1)} all-to-all(f32[8,1,128]{2,1,0:T(1,128)S(1)} %bitcast.15), channel_id=1, replica_groups=mesh['gx'=64,'gy'=8] {'gy'}, dimensions={0} | all-to-all | bytes 8192 | tf_op jit(solution)/shard_map/all_to_all | solution.py:284
  53.1 17.5 %all_to_all.18 = f32[64,1,128]{2,1,0:T(1,128)S(1)} all-to-all(f32[64,1,128]{2,1,0:T(1,128)S(1)} %broadcast_in_dim.2), channel_id=1, replica_groups=mesh['gx'=64,'gy'=8] {'gx'}, dimensions={0} | all-to-all | bytes 65536 | tf_op jit(solution)/shard_map/all_to_all | solution.py:286
  70.5 0.8 %combine.1 = (f32[80,256]{1,0:T(8,128)}, f32[80,256]{1,0:T(8,128)}) custom-call(f32[64,128]{1,0:T(8,128)S(1)} %bitcast.14, f32[218,256]{1,0:T(8,128)S(1)} %get-tuple-element.14.base, f32[180,256]{1,0:T(8,128)S(1)} %first_product.1.own), custom_call_target="tpu_custom_call" | custom-call | tf_op jit(solution)/shard_map/combine/pallas_call | solution.py:287
  (3 shorter events, 0.1 us)
Async XLA Ops:
  1.7 7.6 %collective-permute-start = (f32[29,256]{1,0:T(8,128)S(1)}, f32[29,256]{1,0:T(8,128)S(1)}, u32[]{:S(2)}, u32[]{:S(2)}) collective-permute-start(f32[29,256]{1,0:T(8,128)S(1)} %get-tuple-element.12), channel_id=1, source_target_pairs={{0,1},{1,2},{2,3},{3,4},{4,5},{5,6},{6,7},{7,0},{8,9},{9,10},{10,1... | collective-permute-start | bytes 89096 | tf_op jit(solution)/shard_map/ppermute | solution.py:245
  4.3 5.2 %collective-permute-start.1 = (f32[29,256]{1,0:T(8,128)S(1)}, f32[29,256]{1,0:T(8,128)S(1)}, u32[]{:S(2)}, u32[]{:S(2)}) collective-permute-start(f32[29,256]{1,0:T(8,128)S(1)} %get-tuple-element.13), channel_id=1, source_target_pairs={{1,0},{2,1},{3,2},{4,3},{5,4},{6,5},{7,6},{0,7},{9,8},{10,9},{11,1... | collective-permute-start | bytes 89096 | tf_op jit(solution)/shard_map/ppermute | solution.py:246
  9.5 13.7 %copy-start = (f32[5,5]{1,0:T(8,128)S(1)}, f32[5,5]{1,0:T(8,128)}, u32[]{:S(2)}) copy-start(f32[5,5]{1,0:T(8,128)} %coup_ref.1) | copy-start | bytes 304
  9.5 13.7 %copy-start.1 = (f32[5]{0:T(128)S(1)}, f32[5]{0:T(128)}, u32[]{:S(2)}) copy-start(f32[5]{0:T(128)} %diff_ref.1) | copy-start | bytes 64
  9.5 17.6 %collective-permute-start.3 = (f32[218,256]{1,0:T(8,128)S(1)}, f32[218,256]{1,0:T(8,128)S(1)}, u32[]{:S(2)}, u32[]{:S(2)}) collective-permute-start(f32[218,256]{1,0:T(8,128)S(1)} %get-tuple-element.14.base), channel_id=1, source_target_pairs={{0,504},{8,16},{16,8},{24,32},{32,24},{40,48},{48,40},{56,64},{64,... | collective-permute-start | bytes 669704 | tf_op jit(solution)/shard_map/ppermute | solution.py:261
  21.3 8.6 %collective-permute-start.2 = (f32[218,256]{1,0:T(8,128)S(1)}, f32[218,256]{1,0:T(8,128)S(1)}, u32[]{:S(2)}, u32[]{:S(2)}) collective-permute-start(f32[218,256]{1,0:T(8,128)S(1)} %get-tuple-element.14.base), channel_id=1, source_target_pairs={{0,8},{8,0},{16,24},{24,16},{32,40},{40,32},{48,56},{56,48},{64,72... | collective-permute-start | bytes 669704 | tf_op jit(solution)/shard_map/ppermute | solution.py:262
  30.8 10.2 %collective-permute-start.5 = (f32[180,256]{1,0:T(8,128)S(1)}, f32[180,256]{1,0:T(8,128)S(1)}, u32[]{:S(2)}, u32[]{:S(2)}) collective-permute-start(f32[180,256]{1,0:T(8,128)S(1)} %first_product.1.own), channel_id=1, source_target_pairs={{0,504},{8,16},{16,8},{24,32},{32,24},{40,48},{48,40},{56,64},{64,... | collective-permute-start | bytes 552968 | tf_op jit(solution)/shard_map/ppermute | solution.py:261
  34.4 6.9 %collective-permute-start.4 = (f32[180,256]{1,0:T(8,128)S(1)}, f32[180,256]{1,0:T(8,128)S(1)}, u32[]{:S(2)}, u32[]{:S(2)}) collective-permute-start(f32[180,256]{1,0:T(8,128)S(1)} %first_product.1.own), channel_id=1, source_target_pairs={{0,8},{8,0},{16,24},{24,16},{32,40},{40,32},{48,56},{56,48},{64,72... | collective-permute-start | bytes 552968 | tf_op jit(solution)/shard_map/ppermute | solution.py:262

commit v4 on v3

--- a/solution.py
+++ b/solution.py
@@ -12,6 +12,7 @@
 
 COMPS = 5
 FIELDS = 2 * COMPS
+PLANE_ROWS = 2 * FIELDS + 1
 SUMS = 5
 
 
@@ -74,7 +75,7 @@
     scal[last : last + 1] = jnp.full((1, scal.shape[1]), sign, jnp.float32)
 
 
-def load_kernel(ny, sr, sl, vel, rea, base, coef, low, high, sems):
+def load_kernel(ny, sr, sl, vel, rea, base, coef, sems):
     half = COMPS * ny
     copies = [
         pltpu.make_async_copy(src, dst, sems.at[k])
@@ -92,57 +93,44 @@
         copy.start()
     for copy in copies:
         copy.wait()
+
+
+def edges_kernel(ny, base, even, odd, coef, low, high):
     for out, two, one in ((low, 0, 0), (high, ny - 2, ny - 1)):
+        for plane, ref in enumerate((base, even, odd)):
+            row = plane * PLANE_ROWS
+            for f in range(FIELDS):
+                out[row + 2 * f : row + 2 * f + 2] = ref[f * ny + two : f * ny + two + 2]
+            at = FIELDS * ny + one
+            out[row + 2 * FIELDS : row + 2 * FIELDS + 1] = ref[at : at + 1]
+        row = 3 * PLANE_ROWS
+        for c in range(COMPS + 1):
+            at = (c if c < COMPS else COMPS + 1) * ny + one
+            out[row + c : row + c + 1] = coef[at : at + 1]
+        at = COMPS * ny + two
+        out[row + COMPS + 1 : row + COMPS + 3] = coef[at : at + 2]
+
+
+def first_kernel(ny, scal, coef, lo, hi, base, even, odd, out, field, cext):
+    rows = ny + 8
+    for side, ref in enumerate((base, even, odd)):
+        at = side * PLANE_ROWS
         for f in range(FIELDS):
-            out[2 * f : 2 * f + 2] = base[f * ny + two : f * ny + two + 2]
-        row = 2 * FIELDS
-        for c in range(COMPS):
-            out[row + c : row + c + 1] = coef[c * ny + one : c * ny + one + 1]
-        row += COMPS
-        at = half + ny + one
-        out[row : row + 1] = coef[at : at + 1]
-        at = half + two
-        out[row + 1 : row + 3] = coef[at : at + 2]
-        at = 2 * half + one
-        out[row + 3 : row + 4] = base[at : at + 1]
-
-
-def fill_kernel(ny, base_in, coef_in, lo, hi, base, coef):
-    del base_in, coef_in
-    wide, thin = 2 * FIELDS, COMPS + 3
-    at, last = (FIELDS + 1) * ny, (FIELDS + 1) * ny + 2 * wide
-    base[at : at + wide] = lo[0:wide]
-    base[at + wide : last] = hi[0:wide]
-    base[last : last + 1] = lo[wide + thin : wide + thin + 1]
-    base[last + 1 : last + 2] = hi[wide + thin : wide + thin + 1]
-    at = (COMPS + 2) * ny
-    coef[at : at + thin] = lo[wide : wide + thin]
-    coef[at + thin : at + 2 * thin] = hi[wide : wide + thin]
-
-
-def first_kernel(ny, scal, base, coef, even, odd, out, field, cext):
-    rows = ny + 8
-    for f in range(FIELDS):
-        for side, ref in ((0, base), (1, even), (2, odd)):
             field[side, f, 2 : ny + 2] = ref[f * ny : (f + 1) * ny]
-            at = (FIELDS + 1) * ny + 2 * f
-            field[side, f, 0:2] = ref[at : at + 2]
-            at = at + 2 * FIELDS
-            field[side, f, ny + 2 : ny + 4] = ref[at : at + 2]
-    lo, hi = (COMPS + 2) * ny, (COMPS + 2) * ny + COMPS + 3
-    for c in range(COMPS + 1):
-        at = c * ny if c < COMPS else (COMPS + 1) * ny
-        cext[c, 1 : ny + 1] = coef[at : at + ny]
-        cext[c, 0:1] = coef[lo + c : lo + c + 1]
-        cext[c, ny + 1 : ny + 2] = coef[hi + c : hi + c + 1]
-    at, last = FIELDS * ny, (FIELDS + 1) * ny + 4 * FIELDS
-    for k, ref in ((6, base), (7, even), (8, odd)):
-        cext[k, 1 : ny + 1] = ref[at : at + ny]
-        cext[k, 0:1] = ref[last : last + 1]
-        cext[k, ny + 1 : ny + 2] = ref[last + 1 : last + 2]
+            field[side, f, 0:2] = lo[at + 2 * f : at + 2 * f + 2]
+            field[side, f, ny + 2 : ny + 4] = hi[at + 2 * f : at + 2 * f + 2]
+    for c in range(9):
+        if c < COMPS + 1:
+            at, ref, row = (c if c < COMPS else COMPS + 1) * ny, coef, 3 * PLANE_ROWS + c
+        else:
+            at, ref, row = FIELDS * ny, (base, even, odd)[c - COMPS - 1], (c - COMPS) * PLANE_ROWS - 1
+        cext[c, 1 : ny + 1] = ref[at : at + ny]
+        cext[c, 0:1] = lo[row : row + 1]
+        cext[c, ny + 1 : ny + 2] = hi[row : row + 1]
+    row = 3 * PLANE_ROWS + COMPS + 1
     cext[9, 2 : ny + 2] = coef[COMPS * ny : (COMPS + 1) * ny]
-    cext[9, 0:2] = coef[lo + COMPS + 1 : lo + COMPS + 3]
-    cext[9, ny + 2 : ny + 4] = coef[hi + COMPS + 1 : hi + COMPS + 3]
+    cext[9, 0:2] = lo[row : row + 2]
+    cext[9, ny + 2 : ny + 4] = hi[row : row + 2]
 
     def plane(side):
         return lambda f, shift: field[side, f, 1 + shift : 1 + shift + rows]
@@ -160,18 +148,17 @@
         out[at + 1 : at + 2] = field[0, f, ny + 1 : ny + 2]
 
 
-def second_kernel(ny, copies, scal, base, coef, even1, odd1, own, even, odd, out, field, vys):
+def second_kernel(ny, copies, scal, coef, lo, hi, base, even1, odd1, own, even, odd, out, field, vys):
     for f in range(FIELDS):
         for side, ref in ((0, own), (1, even), (2, odd)):
             field[side, f, 1 : ny + 1] = ref[f * ny : (f + 1) * ny]
             at = FIELDS * ny + 2 * f
             field[side, f, 0:1] = ref[at : at + 1]
             field[side, f, ny + 1 : ny + 2] = ref[at + 1 : at + 2]
-    row = (COMPS + 2) * ny + COMPS + 2
+    row = 3 * PLANE_ROWS + COMPS + 1
     vys[1 : ny + 1] = coef[COMPS * ny : (COMPS + 1) * ny]
-    vys[0:1] = coef[row : row + 1]
-    row += COMPS + 2
-    vys[ny + 1 : ny + 2] = coef[row : row + 1]
+    vys[0:1] = lo[row + 1 : row + 2]
+    vys[ny + 1 : ny + 2] = hi[row : row + 1]
 
     def plane(side):
         return lambda f, shift: field[side, f, 1 + shift : 1 + shift + ny]
@@ -219,18 +206,15 @@
     smem, vmem = pl.BlockSpec(memory_space=pltpu.SMEM), pl.BlockSpec(memory_space=pltpu.VMEM)
     sr, sl, vel, rea = (v.reshape(-1, nz) for v in (right_border, left_border, velocity, reaction))
 
-    base_rows, coef_rows = (FIELDS + 1) * ny + 4 * FIELDS + 2, (COMPS + 2) * ny + 2 * (COMPS + 3)
-    edge_rows = 2 * FIELDS + COMPS + 4
-    base, coef, low, high = pl.pallas_call(
+    base, coef = pl.pallas_call(
         functools.partial(load_kernel, ny),
-        out_shape=[pltpu.VMEM((rows, nz), f32) for rows in (base_rows, coef_rows, edge_rows, edge_rows)],
+        out_shape=[pltpu.VMEM((rows * ny, nz), f32) for rows in (FIELDS + 1, COMPS + 2)],
         in_specs=[pl.BlockSpec(memory_space=pltpu.HBM)] * 4,
-        out_specs=[vmem] * 4,
+        out_specs=[vmem] * 2,
         scratch_shapes=[pltpu.SemaphoreType.DMA((5,))],
         compiler_params=params,
         name="load",
     )(*in_hbm(sr, sl, vel, rea))
-
     scal = pl.pallas_call(
         numbers_kernel,
         out_shape=pltpu.VMEM((32, nz), f32),
@@ -240,47 +224,45 @@
         name="numbers",
     )(coupling, diffusivity)
 
+    even_pairs = [(i, i ^ 1) for i in range(nx_count)]
+    odd_pairs = [(i, (i - 1 if i % 2 == 0 else i + 1) % nx_count) for i in range(nx_count)]
+
+    def swap(v):
+        odd = lax.ppermute(v, "gx", odd_pairs)
+        return lax.ppermute(v, "gx", even_pairs), odd
+
+    even1, odd1 = swap(base)
+    low, high = pl.pallas_call(
+        functools.partial(edges_kernel, ny),
+        out_shape=[pltpu.VMEM((-(-(3 * PLANE_ROWS + COMPS + 3) // 8) * 8, nz), f32)] * 2,
+        in_specs=[vmem] * 4,
+        out_specs=[vmem] * 2,
+        compiler_params=params,
+        name="edges",
+    )(*in_vmem(base, even1, odd1, coef))
     ahead = [(i, (i + 1) % ny_count) for i in range(ny_count)]
     back = [(j, i) for i, j in ahead]
     lo = lax.ppermute(high, "gy", ahead)
     hi = lax.ppermute(low, "gy", back)
-    base, coef = pl.pallas_call(
-        functools.partial(fill_kernel, ny),
-        out_shape=[pltpu.VMEM(base.shape, f32), pltpu.VMEM(coef.shape, f32)],
-        in_specs=[vmem] * 4,
-        out_specs=[vmem] * 2,
-        input_output_aliases={0: 0, 1: 1},
-        compiler_params=params,
-        name="fill",
-    )(*in_vmem(base, coef, lo, hi))
-
-    even_pairs = [(i, i ^ 1) for i in range(nx_count)]
-    odd_pairs = [(i, (i - 1 if i % 2 == 0 else i + 1) % nx_count) for i in range(nx_count)]
-
-    def swap(v):
-        odd = lax.ppermute(v, "gx", odd_pairs)
-        return lax.ppermute(v, "gx", even_pairs), odd
-
-    even1, odd1 = swap(base)
     own = pl.pallas_call(
         functools.partial(first_kernel, ny),
-        out_shape=pltpu.VMEM((FIELDS * (ny + 2), nz), f32),
-        in_specs=[vmem] * 5,
+        out_shape=pltpu.VMEM((-(-FIELDS * (ny + 2) // 8) * 8, nz), f32),
+        in_specs=[vmem] * 7,
         out_specs=vmem,
         scratch_shapes=[pltpu.VMEM((3, FIELDS, ny + 16, nz), f32), pltpu.VMEM((10, ny + 16, nz), f32)],
         compiler_params=params,
         name="first_product",
-    )(*in_vmem(scal, base, coef, even1, odd1))
+    )(*in_vmem(scal, coef, lo, hi, base, even1, odd1))
     even2, odd2 = swap(own)
     shares = pl.pallas_call(
         functools.partial(second_kernel, ny, ny_count),
         out_shape=pltpu.VMEM((ny_count, 128), f32),
-        in_specs=[vmem] * 8,
+        in_specs=[vmem] * 10,
         out_specs=vmem,
         scratch_shapes=[pltpu.VMEM((3, FIELDS, ny + 8, nz), f32), pltpu.VMEM((ny + 8, nz), f32)],
         compiler_params=params,
         name="second_product",
-    )(*in_vmem(scal, base, coef, even1, odd1, own, even2, odd2))
+    )(*in_vmem(scal, coef, lo, hi, base, even1, odd1, own, even2, odd2))
     shares = lax.all_to_all(shares, "gy", 0, 0, tiled=True)
     shares = jnp.broadcast_to(jnp.sum(shares, axis=0, keepdims=True), (nx_count, 128))
     shares = lax.all_to_all(shares, "gx", 0, 0, tiled=True)

time: 71.6 us -> 70.8 us (0.989)
  waiting for transfers between devices: 11.9 us -> 14.4 us
  blocking collectives: 28.4 us -> 26.7 us
  starting transfers between devices: 26.1 us -> 24.5 us
    ppermute x1, starting transfers between devices: 4.3 us -> 0.01 us  [per_device(): hi = lax.ppermute(low, 'gy', back)]
    ppermute x2, starting transfers between devices: 15.4 us -> 17.7 us  [swap(): odd = lax.ppermute(v, 'gx', odd_pairs)]
    ppermute x1, waiting for transfers between devices: 0.18 us -> 2.37 us  [per_device(): hi = lax.ppermute(low, 'gy', back)]
    all_to_all x1, blocking collectives: 11 us -> 9.2 us  [per_device(): shares = lax.all_to_all(shares, 'gy', 0, 0, tiled=True)]
  transfers between devices with their start and end apart: 6 -> 6, of which waited for: 6 -> 5; matrix products, arithmetic and copies ran while one was open for 0% -> 0% of each run, Pallas kernels for 1% -> 1%
where the time goes in v4:
time: 70.8 us; the launch traced here: 70.5 us
  blocking collectives  26.7 us (38%)
  starting transfers between devices  24.5 us (35%)
  waiting for transfers between devices  14.4 us (20%)
  Pallas kernels  4.16 us (6%)
  between operations  0.71 us (1%)
    ppermute x2, starting transfers between devices, swap(): odd = lax.ppermute(v, 'gx', odd_pairs)  17.7 us
    all_to_all x1, blocking collectives, per_device(): shares = lax.all_to_all(shares, 'gx', 0, 0, tiled=True)  17.5 us
    all_to_all x1, blocking collectives, per_device(): shares = lax.all_to_all(shares, 'gy', 0, 0, tiled=True)  9.2 us
    ppermute x2, waiting for transfers between devices, swap(): odd = lax.ppermute(v, 'gx', odd_pairs)  8.49 us
    ppermute x2, starting transfers between devices, swap(): return (lax.ppermute(v, 'gx', even_pairs), odd)  3.84 us
    ppermute x1, starting transfers between devices, per_device(): lo = lax.ppermute(high, 'gy', ahead)  2.97 us
    ppermute x2, waiting for transfers between devices, swap(): return (lax.ppermute(v, 'gx', even_pairs), odd)  2.74 us
    ppermute x1, waiting for transfers between devices, per_device(): hi = lax.ppermute(low, 'gy', back)  2.37 us
  transfers between devices with their start and end apart: 6, of which 5 were waited for; matrix products, arithmetic and copies ran while one was open for 0% of the time, Pallas kernels for 1%

profile of v4, /device:TPU:1, one launch (start us, length us, event | category | flops | bytes accessed | tf_op | source)
XLA Modules:
  0.0 70.5 jit_solution(13882790848805463360)
XLA Ops:
  0.6 1.0 %load.1 = (f32[176,256]{1,0:T(8,128)S(1)}, f32[112,256]{1,0:T(8,128)S(1)}) custom-call(f32[80,256]{1,0:T(8,128)} %bitcast.16, f32[80,256]{1,0:T(8,128)} %bitcast.17, f32[48,256]{1,0:T(8,128)} %bitcast.19, f32[80,256]{1,0:T(8,128)} %bitcast.18), custom_call_target="tpu_custom_call" | custom-call | tf_op jit(solution)/shard_map/load/pallas_call | solution.py:209
  1.7 14.4 %collective-permute-start.1 = (f32[176,256]{1,0:T(8,128)S(1)}, f32[176,256]{1,0:T(8,128)S(1)}, u32[]{:S(2)}, u32[]{:S(2)}) collective-permute-start(f32[176,256]{1,0:T(8,128)S(1)} %get-tuple-element.9.base), channel_id=1, source_target_pairs={{0,504},{8,16},{16,8},{24,32},{32,24},{40,48},{48,40},{56,64},{64,... | collective-permute-start | bytes 540680 | tf_op jit(solution)/shard_map/ppermute | solution.py:231
  16.1 1.9 %collective-permute-start = (f32[176,256]{1,0:T(8,128)S(1)}, f32[176,256]{1,0:T(8,128)S(1)}, u32[]{:S(2)}, u32[]{:S(2)}) collective-permute-start(f32[176,256]{1,0:T(8,128)S(1)} %get-tuple-element.9.base), channel_id=1, source_target_pairs={{0,8},{8,0},{16,24},{24,16},{32,40},{40,32},{48,56},{56,48},{64,72... | collective-permute-start | bytes 540680 | tf_op jit(solution)/shard_map/ppermute | solution.py:232
  18.0 2.3 %collective-permute-done.1.odd.odd1 = f32[176,256]{1,0:T(8,128)S(1)} collective-permute-done((f32[176,256]{1,0:T(8,128)S(1)}, f32[176,256]{1,0:T(8,128)S(1)}, u32[]{:S(2)}, u32[]{:S(2)}) %collective-permute-start.1) | collective-permute-done | bytes 180256 | tf_op jit(solution)/shard_map/ppermute | solution.py:231
  20.3 2.7 %collective-permute-done.even.even1 = f32[176,256]{1,0:T(8,128)S(1)} collective-permute-done((f32[176,256]{1,0:T(8,128)S(1)}, f32[176,256]{1,0:T(8,128)S(1)}, u32[]{:S(2)}, u32[]{:S(2)}) %collective-permute-start) | collective-permute-done | bytes 180256 | tf_op jit(solution)/shard_map/ppermute | solution.py:232
  23.1 0.0 copy-start
  23.1 0.1 edges.1
  23.1 0.0 copy-start.1
  23.2 3.0 %collective-permute-start.2 = (f32[72,256]{1,0:T(8,128)S(1)}, f32[72,256]{1,0:T(8,128)S(1)}, u32[]{:S(2)}, u32[]{:S(2)}) collective-permute-start(f32[72,256]{1,0:T(8,128)S(1)} %get-tuple-element.10), channel_id=1, source_target_pairs={{0,1},{1,2},{2,3},{3,4},{4,5},{5,6},{6,7},{7,0},{8,9},{9,10},{10,1... | collective-permute-start | bytes 221192 | tf_op jit(solution)/shard_map/ppermute | solution.py:245
  26.1 0.0 collective-permute-start.3
  26.1 0.0 copy-done
  26.1 0.0 copy-done.1
  26.1 0.6 numbers.1.scal
  26.8 0.8 %collective-permute-done.2.lo = f32[72,256]{1,0:T(8,128)S(1)} collective-permute-done((f32[72,256]{1,0:T(8,128)S(1)}, f32[72,256]{1,0:T(8,128)S(1)}, u32[]{:S(2)}, u32[]{:S(2)}) %collective-permute-start.2) | collective-permute-done | bytes 73760 | tf_op jit(solution)/shard_map/ppermute | solution.py:245
  27.5 2.4 %collective-permute-done.3.hi = f32[72,256]{1,0:T(8,128)S(1)} collective-permute-done((f32[72,256]{1,0:T(8,128)S(1)}, f32[72,256]{1,0:T(8,128)S(1)}, u32[]{:S(2)}, u32[]{:S(2)}) %collective-permute-start.3) | collective-permute-done | bytes 73760 | tf_op jit(solution)/shard_map/ppermute | solution.py:246
  29.9 0.9 %first_product.1.own = f32[184,256]{1,0:T(8,128)S(1)} custom-call(f32[32,256]{1,0:T(8,128)S(1)} %numbers.1.scal, f32[112,256]{1,0:T(8,128)S(1)} %get-tuple-element.8.coef, f32[72,256]{1,0:T(8,128)S(1)} %collective-permute-done.2.lo, f32[72,256]{1,0:T(8,128)S(1)} %collective-permute-done.3.hi, f32[176,256]{1,0:T(8,128)S(1)} %get-tuple-element.9.base, ...), custom_call_target="tpu_custom_call" | custom-call | tf_op jit(solution)/shard_map/first_product/pallas_call | solution.py:247
  30.8 3.3 %collective-permute-start.5 = (f32[184,256]{1,0:T(8,128)S(1)}, f32[184,256]{1,0:T(8,128)S(1)}, u32[]{:S(2)}, u32[]{:S(2)}) collective-permute-start(f32[184,256]{1,0:T(8,128)S(1)} %first_product.1.own), channel_id=1, source_target_pairs={{0,504},{8,16},{16,8},{24,32},{32,24},{40,48},{48,40},{56,64},{64,... | collective-permute-start | bytes 565256 | tf_op jit(solution)/shard_map/ppermute | solution.py:231
  34.1 1.9 %collective-permute-start.4 = (f32[184,256]{1,0:T(8,128)S(1)}, f32[184,256]{1,0:T(8,128)S(1)}, u32[]{:S(2)}, u32[]{:S(2)}) collective-permute-start(f32[184,256]{1,0:T(8,128)S(1)} %first_product.1.own), channel_id=1, source_target_pairs={{0,8},{8,0},{16,24},{24,16},{32,40},{40,32},{48,56},{56,48},{64,72... | collective-permute-start | bytes 565256 | tf_op jit(solution)/shard_map/ppermute | solution.py:232
  36.0 6.2 %collective-permute-done.5.odd = f32[184,256]{1,0:T(8,128)S(1)} collective-permute-done((f32[184,256]{1,0:T(8,128)S(1)}, f32[184,256]{1,0:T(8,128)S(1)}, u32[]{:S(2)}, u32[]{:S(2)}) %collective-permute-start.5) | collective-permute-done | bytes 188448 | tf_op jit(solution)/shard_map/ppermute | solution.py:231
  42.2 0.0 collective-permute-done.4.even
  42.2 0.8 %second_product.1 = f32[8,128]{1,0:T(8,128)S(1)} custom-call(f32[32,256]{1,0:T(8,128)S(1)} %numbers.1.scal, f32[112,256]{1,0:T(8,128)S(1)} %get-tuple-element.8.coef, f32[72,256]{1,0:T(8,128)S(1)} %collective-permute-done.2.lo, f32[72,256]{1,0:T(8,128)S(1)} %collective-permute-done.3.hi, f32[176,256]{1,0:T(8,128)S(1)} %get-tuple-element.9.base, ...), custom_call_target="tpu_custom_call" | custom-call | tf_op jit(solution)/shard_map/second_product/pallas_call | solution.py:257
  43.0 9.2 %all_to_all.17 = f32[8,1,128]{2,1,0:T(1,128)S(1)} all-to-all(f32[8,1,128]{2,1,0:T(1,128)S(1)} %bitcast.15), channel_id=1, replica_groups=mesh['gx'=64,'gy'=8] {'gy'}, dimensions={0} | all-to-all | bytes 8192 | tf_op jit(solution)/shard_map/all_to_all | solution.py:266
  52.2 17.5 %all_to_all.18 = f32[64,1,128]{2,1,0:T(1,128)S(1)} all-to-all(f32[64,1,128]{2,1,0:T(1,128)S(1)} %broadcast_in_dim.2), channel_id=1, replica_groups=mesh['gx'=64,'gy'=8] {'gx'}, dimensions={0} | all-to-all | bytes 65536 | tf_op jit(solution)/shard_map/all_to_all | solution.py:268
  69.7 0.8 %combine.1 = (f32[80,256]{1,0:T(8,128)}, f32[80,256]{1,0:T(8,128)}) custom-call(f32[64,128]{1,0:T(8,128)S(1)} %bitcast.14, f32[176,256]{1,0:T(8,128)S(1)} %get-tuple-element.9.base, f32[184,256]{1,0:T(8,128)S(1)} %first_product.1.own), custom_call_target="tpu_custom_call" | custom-call | tf_op jit(solution)/shard_map/combine/pallas_call | solution.py:269
  (2 shorter events, 0.0 us)
Async XLA Ops:
  1.7 18.7 %collective-permute-start.1 = (f32[176,256]{1,0:T(8,128)S(1)}, f32[176,256]{1,0:T(8,128)S(1)}, u32[]{:S(2)}, u32[]{:S(2)}) collective-permute-start(f32[176,256]{1,0:T(8,128)S(1)} %get-tuple-element.9.base), channel_id=1, source_target_pairs={{0,504},{8,16},{16,8},{24,32},{32,24},{40,48},{48,40},{56,64},{64,... | collective-permute-start | bytes 540680 | tf_op jit(solution)/shard_map/ppermute | solution.py:231
  16.1 7.0 %collective-permute-start = (f32[176,256]{1,0:T(8,128)S(1)}, f32[176,256]{1,0:T(8,128)S(1)}, u32[]{:S(2)}, u32[]{:S(2)}) collective-permute-start(f32[176,256]{1,0:T(8,128)S(1)} %get-tuple-element.9.base), channel_id=1, source_target_pairs={{0,8},{8,0},{16,24},{24,16},{32,40},{40,32},{48,56},{56,48},{64,72... | collective-permute-start | bytes 540680 | tf_op jit(solution)/shard_map/ppermute | solution.py:232
  23.1 3.1 %copy-start = (f32[5,5]{1,0:T(8,128)S(1)}, f32[5,5]{1,0:T(8,128)}, u32[]{:S(2)}) copy-start(f32[5,5]{1,0:T(8,128)} %coup_ref.1) | copy-start | bytes 304
  23.1 3.0 %copy-start.1 = (f32[5]{0:T(128)S(1)}, f32[5]{0:T(128)}, u32[]{:S(2)}) copy-start(f32[5]{0:T(128)} %diff_ref.1) | copy-start | bytes 64
  23.2 4.4 %collective-permute-start.2 = (f32[72,256]{1,0:T(8,128)S(1)}, f32[72,256]{1,0:T(8,128)S(1)}, u32[]{:S(2)}, u32[]{:S(2)}) collective-permute-start(f32[72,256]{1,0:T(8,128)S(1)} %get-tuple-element.10), channel_id=1, source_target_pairs={{0,1},{1,2},{2,3},{3,4},{4,5},{5,6},{6,7},{7,0},{8,9},{9,10},{10,1... | collective-permute-start | bytes 221192 | tf_op jit(solution)/shard_map/ppermute | solution.py:245
  26.1 3.8 %collective-permute-start.3 = (f32[72,256]{1,0:T(8,128)S(1)}, f32[72,256]{1,0:T(8,128)S(1)}, u32[]{:S(2)}, u32[]{:S(2)}) collective-permute-start(f32[72,256]{1,0:T(8,128)S(1)} %get-tuple-element.11), channel_id=1, source_target_pairs={{1,0},{2,1},{3,2},{4,3},{5,4},{6,5},{7,6},{0,7},{9,8},{10,9},{11,1... | collective-permute-start | bytes 221192 | tf_op jit(solution)/shard_map/ppermute | solution.py:246
  30.8 11.4 %collective-permute-start.5 = (f32[184,256]{1,0:T(8,128)S(1)}, f32[184,256]{1,0:T(8,128)S(1)}, u32[]{:S(2)}, u32[]{:S(2)}) collective-permute-start(f32[184,256]{1,0:T(8,128)S(1)} %first_product.1.own), channel_id=1, source_target_pairs={{0,504},{8,16},{16,8},{24,32},{32,24},{40,48},{48,40},{56,64},{64,... | collective-permute-start | bytes 565256 | tf_op jit(solution)/shard_map/ppermute | solution.py:231
  34.1 8.1 %collective-permute-start.4 = (f32[184,256]{1,0:T(8,128)S(1)}, f32[184,256]{1,0:T(8,128)S(1)}, u32[]{:S(2)}, u32[]{:S(2)}) collective-permute-start(f32[184,256]{1,0:T(8,128)S(1)} %first_product.1.own), channel_id=1, source_target_pairs={{0,8},{8,0},{16,24},{24,16},{32,40},{40,32},{48,56},{56,48},{64,72... | collective-permute-start | bytes 565256 | tf_op jit(solution)/shard_map/ppermute | solution.py:232

commit v5 on v4

--- a/solution.py
+++ b/solution.py
@@ -161,7 +161,8 @@
     vys[ny + 1 : ny + 2] = hi[row : row + 1]
 
     def plane(side):
-        return lambda f, shift: field[side, f, 1 + shift : 1 + shift + ny]
+        ref = (own, even, odd)[side]
+        return lambda f, shift: field[side, f, 1 + shift : 1 + shift + ny] if shift else ref[f * ny : (f + 1) * ny]
 
     at, vz = FIELDS * ny, (COMPS + 1) * ny
     outs = apply_both(
@@ -174,7 +175,7 @@
     for system in range(2):
         sums = [0.0] * SUMS
         for f in range(system * COMPS, (system + 1) * COMPS):
-            s, w1, w2 = base[f * ny : (f + 1) * ny], field[0, f, 1 : ny + 1], outs[f]
+            s, w1, w2 = base[f * ny : (f + 1) * ny], own[f * ny : (f + 1) * ny], outs[f]
             for k, term in enumerate((w1 * w1, w1 * w2, w2 * w2, w1 * s, w2 * s)):
                 sums[k] = sums[k] + term
         for k in range(SUMS):

time: 70.8 us -> 70.6 us (level)
  no operation moved by 1% of the time
where the time goes in v5:
time: 70.6 us; the launch traced here: 70.2 us
  blocking collectives  26.7 us (38%)
  starting transfers between devices  24.5 us (35%)
  waiting for transfers between devices  14.4 us (20%)
  Pallas kernels  3.94 us (6%)
  between operations  0.71 us (1%)
    ppermute x2, starting transfers between devices, swap(): odd = lax.ppermute(v, 'gx', odd_pairs)  17.7 us
    all_to_all x1, blocking collectives, per_device(): shares = lax.all_to_all(shares, 'gx', 0, 0, tiled=True)  17.5 us
    all_to_all x1, blocking collectives, per_device(): shares = lax.all_to_all(shares, 'gy', 0, 0, tiled=True)  9.2 us
    ppermute x2, waiting for transfers between devices, swap(): odd = lax.ppermute(v, 'gx', odd_pairs)  8.49 us
    ppermute x2, starting transfers between devices, swap(): return (lax.ppermute(v, 'gx', even_pairs), odd)  3.84 us
    ppermute x1, starting transfers between devices, per_device(): lo = lax.ppermute(high, 'gy', ahead)  2.97 us
    ppermute x2, waiting for transfers between devices, swap(): return (lax.ppermute(v, 'gx', even_pairs), odd)  2.74 us
    ppermute x1, waiting for transfers between devices, per_device(): hi = lax.ppermute(low, 'gy', back)  2.37 us
  transfers between devices with their start and end apart: 6, of which 5 were waited for; matrix products, arithmetic and copies ran while one was open for 0% of the time, Pallas kernels for 1%

profile of v5, /device:TPU:1, one launch (start us, length us, event | category | flops | bytes accessed | tf_op | source)
XLA Modules:
  0.0 70.2 jit_solution(5175871935067879479)
XLA Ops:
  0.6 1.0 %load.1 = (f32[176,256]{1,0:T(8,128)S(1)}, f32[112,256]{1,0:T(8,128)S(1)}) custom-call(f32[80,256]{1,0:T(8,128)} %bitcast.16, f32[80,256]{1,0:T(8,128)} %bitcast.17, f32[48,256]{1,0:T(8,128)} %bitcast.19, f32[80,256]{1,0:T(8,128)} %bitcast.18), custom_call_target="tpu_custom_call" | custom-call | tf_op jit(solution)/shard_map/load/pallas_call | solution.py:210
  1.7 14.4 %collective-permute-start.1 = (f32[176,256]{1,0:T(8,128)S(1)}, f32[176,256]{1,0:T(8,128)S(1)}, u32[]{:S(2)}, u32[]{:S(2)}) collective-permute-start(f32[176,256]{1,0:T(8,128)S(1)} %get-tuple-element.9.base), channel_id=1, source_target_pairs={{0,504},{8,16},{16,8},{24,32},{32,24},{40,48},{48,40},{56,64},{64,... | collective-permute-start | bytes 540680 | tf_op jit(solution)/shard_map/ppermute | solution.py:232
  16.1 1.9 %collective-permute-start = (f32[176,256]{1,0:T(8,128)S(1)}, f32[176,256]{1,0:T(8,128)S(1)}, u32[]{:S(2)}, u32[]{:S(2)}) collective-permute-start(f32[176,256]{1,0:T(8,128)S(1)} %get-tuple-element.9.base), channel_id=1, source_target_pairs={{0,8},{8,0},{16,24},{24,16},{32,40},{40,32},{48,56},{56,48},{64,72... | collective-permute-start | bytes 540680 | tf_op jit(solution)/shard_map/ppermute | solution.py:233
  18.0 2.3 %collective-permute-done.1.odd.odd1 = f32[176,256]{1,0:T(8,128)S(1)} collective-permute-done((f32[176,256]{1,0:T(8,128)S(1)}, f32[176,256]{1,0:T(8,128)S(1)}, u32[]{:S(2)}, u32[]{:S(2)}) %collective-permute-start.1) | collective-permute-done | bytes 180256 | tf_op jit(solution)/shard_map/ppermute | solution.py:232
  20.3 2.7 %collective-permute-done.even.even1 = f32[176,256]{1,0:T(8,128)S(1)} collective-permute-done((f32[176,256]{1,0:T(8,128)S(1)}, f32[176,256]{1,0:T(8,128)S(1)}, u32[]{:S(2)}, u32[]{:S(2)}) %collective-permute-start) | collective-permute-done | bytes 180256 | tf_op jit(solution)/shard_map/ppermute | solution.py:233
  23.1 0.0 copy-start
  23.1 0.1 edges.1
  23.1 0.0 copy-start.1
  23.2 3.0 %collective-permute-start.2 = (f32[72,256]{1,0:T(8,128)S(1)}, f32[72,256]{1,0:T(8,128)S(1)}, u32[]{:S(2)}, u32[]{:S(2)}) collective-permute-start(f32[72,256]{1,0:T(8,128)S(1)} %get-tuple-element.10), channel_id=1, source_target_pairs={{0,1},{1,2},{2,3},{3,4},{4,5},{5,6},{6,7},{7,0},{8,9},{9,10},{10,1... | collective-permute-start | bytes 221192 | tf_op jit(solution)/shard_map/ppermute | solution.py:246
  26.1 0.0 collective-permute-start.3
  26.1 0.0 copy-done
  26.1 0.0 copy-done.1
  26.1 0.6 numbers.1.scal
  26.8 0.8 %collective-permute-done.2.lo = f32[72,256]{1,0:T(8,128)S(1)} collective-permute-done((f32[72,256]{1,0:T(8,128)S(1)}, f32[72,256]{1,0:T(8,128)S(1)}, u32[]{:S(2)}, u32[]{:S(2)}) %collective-permute-start.2) | collective-permute-done | bytes 73760 | tf_op jit(solution)/shard_map/ppermute | solution.py:246
  27.5 2.4 %collective-permute-done.3.hi = f32[72,256]{1,0:T(8,128)S(1)} collective-permute-done((f32[72,256]{1,0:T(8,128)S(1)}, f32[72,256]{1,0:T(8,128)S(1)}, u32[]{:S(2)}, u32[]{:S(2)}) %collective-permute-start.3) | collective-permute-done | bytes 73760 | tf_op jit(solution)/shard_map/ppermute | solution.py:247
  29.9 0.9 %first_product.1.own = f32[184,256]{1,0:T(8,128)S(1)} custom-call(f32[32,256]{1,0:T(8,128)S(1)} %numbers.1.scal, f32[112,256]{1,0:T(8,128)S(1)} %get-tuple-element.8.coef, f32[72,256]{1,0:T(8,128)S(1)} %collective-permute-done.2.lo, f32[72,256]{1,0:T(8,128)S(1)} %collective-permute-done.3.hi, f32[176,256]{1,0:T(8,128)S(1)} %get-tuple-element.9.base, ...), custom_call_target="tpu_custom_call" | custom-call | tf_op jit(solution)/shard_map/first_product/pallas_call | solution.py:248
  30.8 3.3 %collective-permute-start.5 = (f32[184,256]{1,0:T(8,128)S(1)}, f32[184,256]{1,0:T(8,128)S(1)}, u32[]{:S(2)}, u32[]{:S(2)}) collective-permute-start(f32[184,256]{1,0:T(8,128)S(1)} %first_product.1.own), channel_id=1, source_target_pairs={{0,504},{8,16},{16,8},{24,32},{32,24},{40,48},{48,40},{56,64},{64,... | collective-permute-start | bytes 565256 | tf_op jit(solution)/shard_map/ppermute | solution.py:232
  34.1 1.9 %collective-permute-start.4 = (f32[184,256]{1,0:T(8,128)S(1)}, f32[184,256]{1,0:T(8,128)S(1)}, u32[]{:S(2)}, u32[]{:S(2)}) collective-permute-start(f32[184,256]{1,0:T(8,128)S(1)} %first_product.1.own), channel_id=1, source_target_pairs={{0,8},{8,0},{16,24},{24,16},{32,40},{40,32},{48,56},{56,48},{64,72... | collective-permute-start | bytes 565256 | tf_op jit(solution)/shard_map/ppermute | solution.py:233
  36.0 6.2 %collective-permute-done.5.odd = f32[184,256]{1,0:T(8,128)S(1)} collective-permute-done((f32[184,256]{1,0:T(8,128)S(1)}, f32[184,256]{1,0:T(8,128)S(1)}, u32[]{:S(2)}, u32[]{:S(2)}) %collective-permute-start.5) | collective-permute-done | bytes 188448 | tf_op jit(solution)/shard_map/ppermute | solution.py:232
  42.2 0.0 collective-permute-done.4.even
  42.2 0.6 second_product.1
  42.8 9.2 %all_to_all.17 = f32[8,1,128]{2,1,0:T(1,128)S(1)} all-to-all(f32[8,1,128]{2,1,0:T(1,128)S(1)} %bitcast.15), channel_id=1, replica_groups=mesh['gx'=64,'gy'=8] {'gy'}, dimensions={0} | all-to-all | bytes 8192 | tf_op jit(solution)/shard_map/all_to_all | solution.py:267
  52.0 17.5 %all_to_all.18 = f32[64,1,128]{2,1,0:T(1,128)S(1)} all-to-all(f32[64,1,128]{2,1,0:T(1,128)S(1)} %broadcast_in_dim.2), channel_id=1, replica_groups=mesh['gx'=64,'gy'=8] {'gx'}, dimensions={0} | all-to-all | bytes 65536 | tf_op jit(solution)/shard_map/all_to_all | solution.py:269
  69.5 0.8 %combine.1 = (f32[80,256]{1,0:T(8,128)}, f32[80,256]{1,0:T(8,128)}) custom-call(f32[64,128]{1,0:T(8,128)S(1)} %bitcast.14, f32[176,256]{1,0:T(8,128)S(1)} %get-tuple-element.9.base, f32[184,256]{1,0:T(8,128)S(1)} %first_product.1.own), custom_call_target="tpu_custom_call" | custom-call | tf_op jit(solution)/shard_map/combine/pallas_call | solution.py:270
  (2 shorter events, 0.0 us)
Async XLA Ops:
  1.7 18.7 %collective-permute-start.1 = (f32[176,256]{1,0:T(8,128)S(1)}, f32[176,256]{1,0:T(8,128)S(1)}, u32[]{:S(2)}, u32[]{:S(2)}) collective-permute-start(f32[176,256]{1,0:T(8,128)S(1)} %get-tuple-element.9.base), channel_id=1, source_target_pairs={{0,504},{8,16},{16,8},{24,32},{32,24},{40,48},{48,40},{56,64},{64,... | collective-permute-start | bytes 540680 | tf_op jit(solution)/shard_map/ppermute | solution.py:232
  16.1 7.0 %collective-permute-start = (f32[176,256]{1,0:T(8,128)S(1)}, f32[176,256]{1,0:T(8,128)S(1)}, u32[]{:S(2)}, u32[]{:S(2)}) collective-permute-start(f32[176,256]{1,0:T(8,128)S(1)} %get-tuple-element.9.base), channel_id=1, source_target_pairs={{0,8},{8,0},{16,24},{24,16},{32,40},{40,32},{48,56},{56,48},{64,72... | collective-permute-start | bytes 540680 | tf_op jit(solution)/shard_map/ppermute | solution.py:233
  23.1 3.1 %copy-start = (f32[5,5]{1,0:T(8,128)S(1)}, f32[5,5]{1,0:T(8,128)}, u32[]{:S(2)}) copy-start(f32[5,5]{1,0:T(8,128)} %coup_ref.1) | copy-start | bytes 304
  23.1 3.0 %copy-start.1 = (f32[5]{0:T(128)S(1)}, f32[5]{0:T(128)}, u32[]{:S(2)}) copy-start(f32[5]{0:T(128)} %diff_ref.1) | copy-start | bytes 64
  23.2 4.4 %collective-permute-start.2 = (f32[72,256]{1,0:T(8,128)S(1)}, f32[72,256]{1,0:T(8,128)S(1)}, u32[]{:S(2)}, u32[]{:S(2)}) collective-permute-start(f32[72,256]{1,0:T(8,128)S(1)} %get-tuple-element.10), channel_id=1, source_target_pairs={{0,1},{1,2},{2,3},{3,4},{4,5},{5,6},{6,7},{7,0},{8,9},{9,10},{10,1... | collective-permute-start | bytes 221192 | tf_op jit(solution)/shard_map/ppermute | solution.py:246
  26.1 3.8 %collective-permute-start.3 = (f32[72,256]{1,0:T(8,128)S(1)}, f32[72,256]{1,0:T(8,128)S(1)}, u32[]{:S(2)}, u32[]{:S(2)}) collective-permute-start(f32[72,256]{1,0:T(8,128)S(1)} %get-tuple-element.11), channel_id=1, source_target_pairs={{1,0},{2,1},{3,2},{4,3},{5,4},{6,5},{7,6},{0,7},{9,8},{10,9},{11,1... | collective-permute-start | bytes 221192 | tf_op jit(solution)/shard_map/ppermute | solution.py:247
  30.8 11.4 %collective-permute-start.5 = (f32[184,256]{1,0:T(8,128)S(1)}, f32[184,256]{1,0:T(8,128)S(1)}, u32[]{:S(2)}, u32[]{:S(2)}) collective-permute-start(f32[184,256]{1,0:T(8,128)S(1)} %first_product.1.own), channel_id=1, source_target_pairs={{0,504},{8,16},{16,8},{24,32},{32,24},{40,48},{48,40},{56,64},{64,... | collective-permute-start | bytes 565256 | tf_op jit(solution)/shard_map/ppermute | solution.py:232
  34.1 8.1 %collective-permute-start.4 = (f32[184,256]{1,0:T(8,128)S(1)}, f32[184,256]{1,0:T(8,128)S(1)}, u32[]{:S(2)}, u32[]{:S(2)}) collective-permute-start(f32[184,256]{1,0:T(8,128)S(1)} %first_product.1.own), channel_id=1, source_target_pairs={{0,8},{8,0},{16,24},{24,16},{32,40},{40,32},{48,56},{56,48},{64,72... | collective-permute-start | bytes 565256 | tf_op jit(solution)/shard_map/ppermute | solution.py:233

commit v6 on v5

--- a/solution.py
+++ b/solution.py
@@ -11,6 +11,7 @@
 EDGE = -1.0 / 6.0
 
 COMPS = 5
+SLABS_ALONG_Z = 8
 FIELDS = 2 * COMPS
 PLANE_ROWS = 2 * FIELDS + 1
 SUMS = 5
@@ -264,9 +265,11 @@
         compiler_params=params,
         name="second_product",
     )(*in_vmem(scal, coef, lo, hi, base, even1, odd1, own, even2, odd2))
-    shares = lax.all_to_all(shares, "gy", 0, 0, tiled=True)
+    slabs = sorted(range(nx_count), key=lambda g: (-(g % SLABS_ALONG_Z), abs(g // SLABS_ALONG_Z - SLABS_ALONG_Z // 2)))
+    strips = sorted(range(ny_count), key=lambda g: (5, 7, 3, 4, 6, 1, 2, 0).index(g)) if ny_count == 8 else list(range(ny_count))
+    shares = lax.all_to_all(shares, "gy", 0, 0, tiled=True, axis_index_groups=[strips])
     shares = jnp.broadcast_to(jnp.sum(shares, axis=0, keepdims=True), (nx_count, 128))
-    shares = lax.all_to_all(shares, "gx", 0, 0, tiled=True)
+    shares = lax.all_to_all(shares, "gx", 0, 0, tiled=True, axis_index_groups=[slabs])
     right, left = pl.pallas_call(
         functools.partial(last_kernel, ny),
         out_shape=[jax.ShapeDtypeStruct((comps * ny, nz), f32)] * 2,

time: 70.6 us -> 65.1 us (0.922)
  blocking collectives: 26.7 us -> 20.6 us
    all_to_all x2, blocking collectives: 26.7 us -> 20.6 us  [the longest x1 13.3 us: per_device(): lax.all_to_all(shares, 'gx', 0, 0, tiled=True, axis_index_groups=[slabs])]
where the time goes in v6:
time: 65.1 us; the launch traced here: 64.2 us
  starting transfers between devices  24.5 us (38%)
  blocking collectives  20.6 us (32%)
  waiting for transfers between devices  14.4 us (22%)
  Pallas kernels  3.94 us (6%)
  between operations  0.71 us (1%)
    ppermute x2, starting transfers between devices, swap(): odd = lax.ppermute(v, 'gx', odd_pairs)  17.7 us
    all_to_all x1, blocking collectives, per_device(): lax.all_to_all(shares, 'gx', 0, 0, tiled=True, axis_index_groups=[slabs])  13.3 us
    ppermute x2, waiting for transfers between devices, swap(): odd = lax.ppermute(v, 'gx', odd_pairs)  8.49 us
    all_to_all x1, blocking collectives, per_device(): lax.all_to_all(shares, 'gy', 0, 0, tiled=True, axis_index_groups=[strips])  7.25 us
    ppermute x2, starting transfers between devices, swap(): return (lax.ppermute(v, 'gx', even_pairs), odd)  3.84 us
    ppermute x1, starting transfers between devices, per_device(): lo = lax.ppermute(high, 'gy', ahead)  2.97 us
    ppermute x2, waiting for transfers between devices, swap(): return (lax.ppermute(v, 'gx', even_pairs), odd)  2.74 us
    ppermute x1, waiting for transfers between devices, per_device(): hi = lax.ppermute(low, 'gy', back)  2.37 us
  transfers between devices with their start and end apart: 6, of which 5 were waited for; matrix products, arithmetic and copies ran while one was open for 0% of the time, Pallas kernels for 1%

profile of v6, /device:TPU:1, one launch (start us, length us, event | category | flops | bytes accessed | tf_op | source)
XLA Modules:
  0.0 64.2 jit_solution(7595353576226549969)
XLA Ops:
  0.6 1.0 %load.1 = (f32[176,256]{1,0:T(8,128)S(1)}, f32[112,256]{1,0:T(8,128)S(1)}) custom-call(f32[80,256]{1,0:T(8,128)} %bitcast.16, f32[80,256]{1,0:T(8,128)} %bitcast.17, f32[48,256]{1,0:T(8,128)} %bitcast.19, f32[80,256]{1,0:T(8,128)} %bitcast.18), custom_call_target="tpu_custom_call" | custom-call | tf_op jit(solution)/shard_map/load/pallas_call | solution.py:211
  1.7 14.4 %collective-permute-start.1 = (f32[176,256]{1,0:T(8,128)S(1)}, f32[176,256]{1,0:T(8,128)S(1)}, u32[]{:S(2)}, u32[]{:S(2)}) collective-permute-start(f32[176,256]{1,0:T(8,128)S(1)} %get-tuple-element.9.base), channel_id=1, source_target_pairs={{0,504},{8,16},{16,8},{24,32},{32,24},{40,48},{48,40},{56,64},{64,... | collective-permute-start | bytes 540680 | tf_op jit(solution)/shard_map/ppermute | solution.py:233
  16.1 1.9 %collective-permute-start = (f32[176,256]{1,0:T(8,128)S(1)}, f32[176,256]{1,0:T(8,128)S(1)}, u32[]{:S(2)}, u32[]{:S(2)}) collective-permute-start(f32[176,256]{1,0:T(8,128)S(1)} %get-tuple-element.9.base), channel_id=1, source_target_pairs={{0,8},{8,0},{16,24},{24,16},{32,40},{40,32},{48,56},{56,48},{64,72... | collective-permute-start | bytes 540680 | tf_op jit(solution)/shard_map/ppermute | solution.py:234
  18.0 2.3 %collective-permute-done.1.odd.odd1 = f32[176,256]{1,0:T(8,128)S(1)} collective-permute-done((f32[176,256]{1,0:T(8,128)S(1)}, f32[176,256]{1,0:T(8,128)S(1)}, u32[]{:S(2)}, u32[]{:S(2)}) %collective-permute-start.1) | collective-permute-done | bytes 180256 | tf_op jit(solution)/shard_map/ppermute | solution.py:233
  20.3 2.7 %collective-permute-done.even.even1 = f32[176,256]{1,0:T(8,128)S(1)} collective-permute-done((f32[176,256]{1,0:T(8,128)S(1)}, f32[176,256]{1,0:T(8,128)S(1)}, u32[]{:S(2)}, u32[]{:S(2)}) %collective-permute-start) | collective-permute-done | bytes 180256 | tf_op jit(solution)/shard_map/ppermute | solution.py:234
  23.1 0.0 copy-start
  23.1 0.1 edges.1
  23.1 0.0 copy-start.1
  23.2 3.0 %collective-permute-start.2 = (f32[72,256]{1,0:T(8,128)S(1)}, f32[72,256]{1,0:T(8,128)S(1)}, u32[]{:S(2)}, u32[]{:S(2)}) collective-permute-start(f32[72,256]{1,0:T(8,128)S(1)} %get-tuple-element.10), channel_id=1, source_target_pairs={{0,1},{1,2},{2,3},{3,4},{4,5},{5,6},{6,7},{7,0},{8,9},{9,10},{10,1... | collective-permute-start | bytes 221192 | tf_op jit(solution)/shard_map/ppermute | solution.py:247
  26.1 0.0 collective-permute-start.3
  26.1 0.0 copy-done
  26.1 0.0 copy-done.1
  26.1 0.6 numbers.1.scal
  26.8 0.8 %collective-permute-done.2.lo = f32[72,256]{1,0:T(8,128)S(1)} collective-permute-done((f32[72,256]{1,0:T(8,128)S(1)}, f32[72,256]{1,0:T(8,128)S(1)}, u32[]{:S(2)}, u32[]{:S(2)}) %collective-permute-start.2) | collective-permute-done | bytes 73760 | tf_op jit(solution)/shard_map/ppermute | solution.py:247
  27.5 2.4 %collective-permute-done.3.hi = f32[72,256]{1,0:T(8,128)S(1)} collective-permute-done((f32[72,256]{1,0:T(8,128)S(1)}, f32[72,256]{1,0:T(8,128)S(1)}, u32[]{:S(2)}, u32[]{:S(2)}) %collective-permute-start.3) | collective-permute-done | bytes 73760 | tf_op jit(solution)/shard_map/ppermute | solution.py:248
  29.9 0.9 %first_product.1.own = f32[184,256]{1,0:T(8,128)S(1)} custom-call(f32[32,256]{1,0:T(8,128)S(1)} %numbers.1.scal, f32[112,256]{1,0:T(8,128)S(1)} %get-tuple-element.8.coef, f32[72,256]{1,0:T(8,128)S(1)} %collective-permute-done.2.lo, f32[72,256]{1,0:T(8,128)S(1)} %collective-permute-done.3.hi, f32[176,256]{1,0:T(8,128)S(1)} %get-tuple-element.9.base, ...), custom_call_target="tpu_custom_call" | custom-call | tf_op jit(solution)/shard_map/first_product/pallas_call | solution.py:249
  30.8 3.3 %collective-permute-start.5 = (f32[184,256]{1,0:T(8,128)S(1)}, f32[184,256]{1,0:T(8,128)S(1)}, u32[]{:S(2)}, u32[]{:S(2)}) collective-permute-start(f32[184,256]{1,0:T(8,128)S(1)} %first_product.1.own), channel_id=1, source_target_pairs={{0,504},{8,16},{16,8},{24,32},{32,24},{40,48},{48,40},{56,64},{64,... | collective-permute-start | bytes 565256 | tf_op jit(solution)/shard_map/ppermute | solution.py:233
  34.1 1.9 %collective-permute-start.4 = (f32[184,256]{1,0:T(8,128)S(1)}, f32[184,256]{1,0:T(8,128)S(1)}, u32[]{:S(2)}, u32[]{:S(2)}) collective-permute-start(f32[184,256]{1,0:T(8,128)S(1)} %first_product.1.own), channel_id=1, source_target_pairs={{0,8},{8,0},{16,24},{24,16},{32,40},{40,32},{48,56},{56,48},{64,72... | collective-permute-start | bytes 565256 | tf_op jit(solution)/shard_map/ppermute | solution.py:234
  36.0 6.2 %collective-permute-done.5.odd = f32[184,256]{1,0:T(8,128)S(1)} collective-permute-done((f32[184,256]{1,0:T(8,128)S(1)}, f32[184,256]{1,0:T(8,128)S(1)}, u32[]{:S(2)}, u32[]{:S(2)}) %collective-permute-start.5) | collective-permute-done | bytes 188448 | tf_op jit(solution)/shard_map/ppermute | solution.py:233
  42.2 0.0 collective-permute-done.4.even
  42.2 0.6 second_product.1
  42.8 7.3 %all_to_all.17 = f32[8,1,128]{2,1,0:T(1,128)S(1)} all-to-all(f32[8,1,128]{2,1,0:T(1,128)S(1)} %bitcast.15), channel_id=1, replica_groups={{5,7,3,4,6,1,2,0},{13,15,11,12,14,9,10,8},{21,23,19,20,22,17,18,16},{29..., dimensions={0} | all-to-all | bytes 8192 | tf_op jit(solution)/shard_map/all_to_all | solution.py:270
  50.1 13.3 %all_to_all.18 = f32[64,1,128]{2,1,0:T(1,128)S(1)} all-to-all(f32[64,1,128]{2,1,0:T(1,128)S(1)} %broadcast_in_dim.2), channel_id=1, replica_groups={{312,248,376,184,440,120,504,56,304,240,368,176,432,112,496,48,296,232,..., dimensions={0} | all-to-all | bytes 65536 | tf_op jit(solution)/shard_map/all_to_all | solution.py:272
  63.4 0.8 %combine.1 = (f32[80,256]{1,0:T(8,128)}, f32[80,256]{1,0:T(8,128)}) custom-call(f32[64,128]{1,0:T(8,128)S(1)} %bitcast.14, f32[176,256]{1,0:T(8,128)S(1)} %get-tuple-element.9.base, f32[184,256]{1,0:T(8,128)S(1)} %first_product.1.own), custom_call_target="tpu_custom_call" | custom-call | tf_op jit(solution)/shard_map/combine/pallas_call | solution.py:273
  (2 shorter events, 0.0 us)
Async XLA Ops:
  1.7 18.7 %collective-permute-start.1 = (f32[176,256]{1,0:T(8,128)S(1)}, f32[176,256]{1,0:T(8,128)S(1)}, u32[]{:S(2)}, u32[]{:S(2)}) collective-permute-start(f32[176,256]{1,0:T(8,128)S(1)} %get-tuple-element.9.base), channel_id=1, source_target_pairs={{0,504},{8,16},{16,8},{24,32},{32,24},{40,48},{48,40},{56,64},{64,... | collective-permute-start | bytes 540680 | tf_op jit(solution)/shard_map/ppermute | solution.py:233
  16.1 7.0 %collective-permute-start = (f32[176,256]{1,0:T(8,128)S(1)}, f32[176,256]{1,0:T(8,128)S(1)}, u32[]{:S(2)}, u32[]{:S(2)}) collective-permute-start(f32[176,256]{1,0:T(8,128)S(1)} %get-tuple-element.9.base), channel_id=1, source_target_pairs={{0,8},{8,0},{16,24},{24,16},{32,40},{40,32},{48,56},{56,48},{64,72... | collective-permute-start | bytes 540680 | tf_op jit(solution)/shard_map/ppermute | solution.py:234
  23.1 3.1 %copy-start = (f32[5,5]{1,0:T(8,128)S(1)}, f32[5,5]{1,0:T(8,128)}, u32[]{:S(2)}) copy-start(f32[5,5]{1,0:T(8,128)} %coup_ref.1) | copy-start | bytes 304
  23.1 3.0 %copy-start.1 = (f32[5]{0:T(128)S(1)}, f32[5]{0:T(128)}, u32[]{:S(2)}) copy-start(f32[5]{0:T(128)} %diff_ref.1) | copy-start | bytes 64
  23.2 4.4 %collective-permute-start.2 = (f32[72,256]{1,0:T(8,128)S(1)}, f32[72,256]{1,0:T(8,128)S(1)}, u32[]{:S(2)}, u32[]{:S(2)}) collective-permute-start(f32[72,256]{1,0:T(8,128)S(1)} %get-tuple-element.10), channel_id=1, source_target_pairs={{0,1},{1,2},{2,3},{3,4},{4,5},{5,6},{6,7},{7,0},{8,9},{9,10},{10,1... | collective-permute-start | bytes 221192 | tf_op jit(solution)/shard_map/ppermute | solution.py:247
  26.1 3.8 %collective-permute-start.3 = (f32[72,256]{1,0:T(8,128)S(1)}, f32[72,256]{1,0:T(8,128)S(1)}, u32[]{:S(2)}, u32[]{:S(2)}) collective-permute-start(f32[72,256]{1,0:T(8,128)S(1)} %get-tuple-element.11), channel_id=1, source_target_pairs={{1,0},{2,1},{3,2},{4,3},{5,4},{6,5},{7,6},{0,7},{9,8},{10,9},{11,1... | collective-permute-start | bytes 221192 | tf_op jit(solution)/shard_map/ppermute | solution.py:248
  30.8 11.4 %collective-permute-start.5 = (f32[184,256]{1,0:T(8,128)S(1)}, f32[184,256]{1,0:T(8,128)S(1)}, u32[]{:S(2)}, u32[]{:S(2)}) collective-permute-start(f32[184,256]{1,0:T(8,128)S(1)} %first_product.1.own), channel_id=1, source_target_pairs={{0,504},{8,16},{16,8},{24,32},{32,24},{40,48},{48,40},{56,64},{64,... | collective-permute-start | bytes 565256 | tf_op jit(solution)/shard_map/ppermute | solution.py:233
  34.1 8.1 %collective-permute-start.4 = (f32[184,256]{1,0:T(8,128)S(1)}, f32[184,256]{1,0:T(8,128)S(1)}, u32[]{:S(2)}, u32[]{:S(2)}) collective-permute-start(f32[184,256]{1,0:T(8,128)S(1)} %first_product.1.own), channel_id=1, source_target_pairs={{0,8},{8,0},{16,24},{24,16},{32,40},{40,32},{48,56},{56,48},{64,72... | collective-permute-start | bytes 565256 | tf_op jit(solution)/shard_map/ppermute | solution.py:234

commit v7 on v6

--- a/solution.py
+++ b/solution.py
@@ -151,11 +151,13 @@
 
 def second_kernel(ny, copies, scal, coef, lo, hi, base, even1, odd1, own, even, odd, out, field, vys):
     for f in range(FIELDS):
-        for side, ref in ((0, own), (1, even), (2, odd)):
-            field[side, f, 1 : ny + 1] = ref[f * ny : (f + 1) * ny]
-            at = FIELDS * ny + 2 * f
-            field[side, f, 0:1] = ref[at : at + 1]
-            field[side, f, ny + 1 : ny + 2] = ref[at + 1 : at + 2]
+        at, block = FIELDS * ny + 2 * f, slice(f * ny, (f + 1) * ny)
+        field[0, f, 1 : ny + 1] = own[block]
+        field[0, f, 0:1] = own[at : at + 1]
+        field[0, f, ny + 1 : ny + 2] = own[at + 1 : at + 2]
+        field[1, f, 1 : ny + 1] = even[block] + odd[block]
+        field[1, f, 0:1] = even[at : at + 1] + odd[at : at + 1]
+        field[1, f, ny + 1 : ny + 2] = even[at + 1 : at + 2] + odd[at + 1 : at + 2]
     row = 3 * PLANE_ROWS + COMPS + 1
     vys[1 : ny + 1] = coef[COMPS * ny : (COMPS + 1) * ny]
     vys[0:1] = lo[row + 1 : row + 2]
@@ -163,6 +165,8 @@
 
     def plane(side):
         ref = (own, even, odd)[side]
+        if side == 2:
+            return lambda f, shift: 0.0 if shift else ref[f * ny : (f + 1) * ny]
         return lambda f, shift: field[side, f, 1 + shift : 1 + shift + ny] if shift else ref[f * ny : (f + 1) * ny]
 
     at, vz = FIELDS * ny, (COMPS + 1) * ny
@@ -261,7 +265,7 @@
         out_shape=pltpu.VMEM((ny_count, 128), f32),
         in_specs=[vmem] * 10,
         out_specs=vmem,
-        scratch_shapes=[pltpu.VMEM((3, FIELDS, ny + 8, nz), f32), pltpu.VMEM((ny + 8, nz), f32)],
+        scratch_shapes=[pltpu.VMEM((2, FIELDS, ny + 8, nz), f32), pltpu.VMEM((ny + 8, nz), f32)],
         compiler_params=params,
         name="second_product",
     )(*in_vmem(scal, coef, lo, hi, base, even1, odd1, own, even2, odd2))

time: 65.1 us -> 65.1 us (level)
  no operation moved by 1% of the time
where the time goes in v7:
time: 65.1 us; the launch traced here: 64.1 us
  starting transfers between devices  24.5 us (38%)
  blocking collectives  20.6 us (32%)
  waiting for transfers between devices  14.4 us (22%)
  Pallas kernels  3.92 us (6%)
  between operations  0.71 us (1%)
    ppermute x2, starting transfers between devices, swap(): odd = lax.ppermute(v, 'gx', odd_pairs)  17.7 us
    all_to_all x1, blocking collectives, per_device(): lax.all_to_all(shares, 'gx', 0, 0, tiled=True, axis_index_groups=[slabs])  13.3 us
    ppermute x2, waiting for transfers between devices, swap(): odd = lax.ppermute(v, 'gx', odd_pairs)  8.49 us
    all_to_all x1, blocking collectives, per_device(): lax.all_to_all(shares, 'gy', 0, 0, tiled=True, axis_index_groups=[strips])  7.25 us
    ppermute x2, starting transfers between devices, swap(): return (lax.ppermute(v, 'gx', even_pairs), odd)  3.84 us
    ppermute x1, starting transfers between devices, per_device(): lo = lax.ppermute(high, 'gy', ahead)  2.97 us
    ppermute x2, waiting for transfers between devices, swap(): return (lax.ppermute(v, 'gx', even_pairs), odd)  2.74 us
    ppermute x1, waiting for transfers between devices, per_device(): hi = lax.ppermute(low, 'gy', back)  2.37 us
  transfers between devices with their start and end apart: 6, of which 5 were waited for; matrix products, arithmetic and copies ran while one was open for 0% of the time, Pallas kernels for 1%

profile of v7, /device:TPU:1, one launch (start us, length us, event | category | flops | bytes accessed | tf_op | source)
XLA Modules:
  0.0 64.1 jit_solution(11601878474024268936)
XLA Ops:
  0.6 1.0 %load.1 = (f32[176,256]{1,0:T(8,128)S(1)}, f32[112,256]{1,0:T(8,128)S(1)}) custom-call(f32[80,256]{1,0:T(8,128)} %bitcast.16, f32[80,256]{1,0:T(8,128)} %bitcast.17, f32[48,256]{1,0:T(8,128)} %bitcast.19, f32[80,256]{1,0:T(8,128)} %bitcast.18), custom_call_target="tpu_custom_call" | custom-call | tf_op jit(solution)/shard_map/load/pallas_call | solution.py:215
  1.7 14.4 %collective-permute-start.1 = (f32[176,256]{1,0:T(8,128)S(1)}, f32[176,256]{1,0:T(8,128)S(1)}, u32[]{:S(2)}, u32[]{:S(2)}) collective-permute-start(f32[176,256]{1,0:T(8,128)S(1)} %get-tuple-element.9.base), channel_id=1, source_target_pairs={{0,504},{8,16},{16,8},{24,32},{32,24},{40,48},{48,40},{56,64},{64,... | collective-permute-start | bytes 540680 | tf_op jit(solution)/shard_map/ppermute | solution.py:237
  16.1 1.9 %collective-permute-start = (f32[176,256]{1,0:T(8,128)S(1)}, f32[176,256]{1,0:T(8,128)S(1)}, u32[]{:S(2)}, u32[]{:S(2)}) collective-permute-start(f32[176,256]{1,0:T(8,128)S(1)} %get-tuple-element.9.base), channel_id=1, source_target_pairs={{0,8},{8,0},{16,24},{24,16},{32,40},{40,32},{48,56},{56,48},{64,72... | collective-permute-start | bytes 540680 | tf_op jit(solution)/shard_map/ppermute | solution.py:238
  18.0 2.3 %collective-permute-done.1.odd.odd1 = f32[176,256]{1,0:T(8,128)S(1)} collective-permute-done((f32[176,256]{1,0:T(8,128)S(1)}, f32[176,256]{1,0:T(8,128)S(1)}, u32[]{:S(2)}, u32[]{:S(2)}) %collective-permute-start.1) | collective-permute-done | bytes 180256 | tf_op jit(solution)/shard_map/ppermute | solution.py:237
  20.3 2.7 %collective-permute-done.even.even1 = f32[176,256]{1,0:T(8,128)S(1)} collective-permute-done((f32[176,256]{1,0:T(8,128)S(1)}, f32[176,256]{1,0:T(8,128)S(1)}, u32[]{:S(2)}, u32[]{:S(2)}) %collective-permute-start) | collective-permute-done | bytes 180256 | tf_op jit(solution)/shard_map/ppermute | solution.py:238
  23.1 0.0 copy-start
  23.1 0.1 edges.1
  23.1 0.0 copy-start.1
  23.2 3.0 %collective-permute-start.2 = (f32[72,256]{1,0:T(8,128)S(1)}, f32[72,256]{1,0:T(8,128)S(1)}, u32[]{:S(2)}, u32[]{:S(2)}) collective-permute-start(f32[72,256]{1,0:T(8,128)S(1)} %get-tuple-element.10), channel_id=1, source_target_pairs={{0,1},{1,2},{2,3},{3,4},{4,5},{5,6},{6,7},{7,0},{8,9},{9,10},{10,1... | collective-permute-start | bytes 221192 | tf_op jit(solution)/shard_map/ppermute | solution.py:251
  26.1 0.0 collective-permute-start.3
  26.1 0.0 copy-done
  26.1 0.0 copy-done.1
  26.1 0.6 numbers.1.scal
  26.8 0.8 %collective-permute-done.2.lo = f32[72,256]{1,0:T(8,128)S(1)} collective-permute-done((f32[72,256]{1,0:T(8,128)S(1)}, f32[72,256]{1,0:T(8,128)S(1)}, u32[]{:S(2)}, u32[]{:S(2)}) %collective-permute-start.2) | collective-permute-done | bytes 73760 | tf_op jit(solution)/shard_map/ppermute | solution.py:251
  27.5 2.4 %collective-permute-done.3.hi = f32[72,256]{1,0:T(8,128)S(1)} collective-permute-done((f32[72,256]{1,0:T(8,128)S(1)}, f32[72,256]{1,0:T(8,128)S(1)}, u32[]{:S(2)}, u32[]{:S(2)}) %collective-permute-start.3) | collective-permute-done | bytes 73760 | tf_op jit(solution)/shard_map/ppermute | solution.py:252
  29.9 0.9 %first_product.1.own = f32[184,256]{1,0:T(8,128)S(1)} custom-call(f32[32,256]{1,0:T(8,128)S(1)} %numbers.1.scal, f32[112,256]{1,0:T(8,128)S(1)} %get-tuple-element.8.coef, f32[72,256]{1,0:T(8,128)S(1)} %collective-permute-done.2.lo, f32[72,256]{1,0:T(8,128)S(1)} %collective-permute-done.3.hi, f32[176,256]{1,0:T(8,128)S(1)} %get-tuple-element.9.base, ...), custom_call_target="tpu_custom_call" | custom-call | tf_op jit(solution)/shard_map/first_product/pallas_call | solution.py:253
  30.8 3.3 %collective-permute-start.5 = (f32[184,256]{1,0:T(8,128)S(1)}, f32[184,256]{1,0:T(8,128)S(1)}, u32[]{:S(2)}, u32[]{:S(2)}) collective-permute-start(f32[184,256]{1,0:T(8,128)S(1)} %first_product.1.own), channel_id=1, source_target_pairs={{0,504},{8,16},{16,8},{24,32},{32,24},{40,48},{48,40},{56,64},{64,... | collective-permute-start | bytes 565256 | tf_op jit(solution)/shard_map/ppermute | solution.py:237
  34.1 1.9 %collective-permute-start.4 = (f32[184,256]{1,0:T(8,128)S(1)}, f32[184,256]{1,0:T(8,128)S(1)}, u32[]{:S(2)}, u32[]{:S(2)}) collective-permute-start(f32[184,256]{1,0:T(8,128)S(1)} %first_product.1.own), channel_id=1, source_target_pairs={{0,8},{8,0},{16,24},{24,16},{32,40},{40,32},{48,56},{56,48},{64,72... | collective-permute-start | bytes 565256 | tf_op jit(solution)/shard_map/ppermute | solution.py:238
  36.0 6.2 %collective-permute-done.5.odd = f32[184,256]{1,0:T(8,128)S(1)} collective-permute-done((f32[184,256]{1,0:T(8,128)S(1)}, f32[184,256]{1,0:T(8,128)S(1)}, u32[]{:S(2)}, u32[]{:S(2)}) %collective-permute-start.5) | collective-permute-done | bytes 188448 | tf_op jit(solution)/shard_map/ppermute | solution.py:237
  42.2 0.0 collective-permute-done.4.even
  42.2 0.5 second_product.1
  42.7 7.3 %all_to_all.17 = f32[8,1,128]{2,1,0:T(1,128)S(1)} all-to-all(f32[8,1,128]{2,1,0:T(1,128)S(1)} %bitcast.15), channel_id=1, replica_groups={{5,7,3,4,6,1,2,0},{13,15,11,12,14,9,10,8},{21,23,19,20,22,17,18,16},{29..., dimensions={0} | all-to-all | bytes 8192 | tf_op jit(solution)/shard_map/all_to_all | solution.py:274
  50.0 13.3 %all_to_all.18 = f32[64,1,128]{2,1,0:T(1,128)S(1)} all-to-all(f32[64,1,128]{2,1,0:T(1,128)S(1)} %broadcast_in_dim.2), channel_id=1, replica_groups={{312,248,376,184,440,120,504,56,304,240,368,176,432,112,496,48,296,232,..., dimensions={0} | all-to-all | bytes 65536 | tf_op jit(solution)/shard_map/all_to_all | solution.py:276
  63.4 0.8 %combine.1 = (f32[80,256]{1,0:T(8,128)}, f32[80,256]{1,0:T(8,128)}) custom-call(f32[64,128]{1,0:T(8,128)S(1)} %bitcast.14, f32[176,256]{1,0:T(8,128)S(1)} %get-tuple-element.9.base, f32[184,256]{1,0:T(8,128)S(1)} %first_product.1.own), custom_call_target="tpu_custom_call" | custom-call | tf_op jit(solution)/shard_map/combine/pallas_call | solution.py:277
  (2 shorter events, 0.0 us)
Async XLA Ops:
  1.7 18.7 %collective-permute-start.1 = (f32[176,256]{1,0:T(8,128)S(1)}, f32[176,256]{1,0:T(8,128)S(1)}, u32[]{:S(2)}, u32[]{:S(2)}) collective-permute-start(f32[176,256]{1,0:T(8,128)S(1)} %get-tuple-element.9.base), channel_id=1, source_target_pairs={{0,504},{8,16},{16,8},{24,32},{32,24},{40,48},{48,40},{56,64},{64,... | collective-permute-start | bytes 540680 | tf_op jit(solution)/shard_map/ppermute | solution.py:237
  16.1 7.0 %collective-permute-start = (f32[176,256]{1,0:T(8,128)S(1)}, f32[176,256]{1,0:T(8,128)S(1)}, u32[]{:S(2)}, u32[]{:S(2)}) collective-permute-start(f32[176,256]{1,0:T(8,128)S(1)} %get-tuple-element.9.base), channel_id=1, source_target_pairs={{0,8},{8,0},{16,24},{24,16},{32,40},{40,32},{48,56},{56,48},{64,72... | collective-permute-start | bytes 540680 | tf_op jit(solution)/shard_map/ppermute | solution.py:238
  23.1 3.1 %copy-start = (f32[5,5]{1,0:T(8,128)S(1)}, f32[5,5]{1,0:T(8,128)}, u32[]{:S(2)}) copy-start(f32[5,5]{1,0:T(8,128)} %coup_ref.1) | copy-start | bytes 304
  23.1 3.0 %copy-start.1 = (f32[5]{0:T(128)S(1)}, f32[5]{0:T(128)}, u32[]{:S(2)}) copy-start(f32[5]{0:T(128)} %diff_ref.1) | copy-start | bytes 64
  23.2 4.4 %collective-permute-start.2 = (f32[72,256]{1,0:T(8,128)S(1)}, f32[72,256]{1,0:T(8,128)S(1)}, u32[]{:S(2)}, u32[]{:S(2)}) collective-permute-start(f32[72,256]{1,0:T(8,128)S(1)} %get-tuple-element.10), channel_id=1, source_target_pairs={{0,1},{1,2},{2,3},{3,4},{4,5},{5,6},{6,7},{7,0},{8,9},{9,10},{10,1... | collective-permute-start | bytes 221192 | tf_op jit(solution)/shard_map/ppermute | solution.py:251
  26.1 3.8 %collective-permute-start.3 = (f32[72,256]{1,0:T(8,128)S(1)}, f32[72,256]{1,0:T(8,128)S(1)}, u32[]{:S(2)}, u32[]{:S(2)}) collective-permute-start(f32[72,256]{1,0:T(8,128)S(1)} %get-tuple-element.11), channel_id=1, source_target_pairs={{1,0},{2,1},{3,2},{4,3},{5,4},{6,5},{7,6},{0,7},{9,8},{10,9},{11,1... | collective-permute-start | bytes 221192 | tf_op jit(solution)/shard_map/ppermute | solution.py:252
  30.8 11.4 %collective-permute-start.5 = (f32[184,256]{1,0:T(8,128)S(1)}, f32[184,256]{1,0:T(8,128)S(1)}, u32[]{:S(2)}, u32[]{:S(2)}) collective-permute-start(f32[184,256]{1,0:T(8,128)S(1)} %first_product.1.own), channel_id=1, source_target_pairs={{0,504},{8,16},{16,8},{24,32},{32,24},{40,48},{48,40},{56,64},{64,... | collective-permute-start | bytes 565256 | tf_op jit(solution)/shard_map/ppermute | solution.py:237
  34.1 8.1 %collective-permute-start.4 = (f32[184,256]{1,0:T(8,128)S(1)}, f32[184,256]{1,0:T(8,128)S(1)}, u32[]{:S(2)}, u32[]{:S(2)}) collective-permute-start(f32[184,256]{1,0:T(8,128)S(1)} %first_product.1.own), channel_id=1, source_target_pairs={{0,8},{8,0},{16,24},{24,16},{32,40},{40,32},{48,56},{56,48},{64,72... | collective-permute-start | bytes 565256 | tf_op jit(solution)/shard_map/ppermute | solution.py:238
